TPU v7x, 32 devices: a whole 2x2x4 slice. The times are simulated.
32 devices in a mesh: gx: 4 (over y, x), gy: 2 (over core), gz: 4 (over z).
Axes of the slice: x: 2, y: 2, z: 4, core: 2. Of those that a mesh axis runs over, the one named last changes fastest.
Arguments:
- features: bfloat16 [32, 32, 64, 512], P(None, 'gx', 'gy', 'gz'), may hold values from -12 to 12
- posteriors: bfloat16 [16, 32, 64, 512], P(None, 'gx', 'gy', 'gz'), may hold values from 0 to 1, as said below
Outputs:
- segmentation: bfloat16 [16, 32, 64, 512], P(None, 'gx', 'gy', 'gz')
- class_means: float32 [16, 32], replicated
Inputs may be any that keep to these rules, and one draw needn't show every extreme that they name: Each voxel's 16 initial posteriors are positive and sum to one up to rounding.
All inputs are finite; a program needn't handle non-finite values.
Results may differ from a plain program's by a relative error of at most 0.0075.
Values may be sent and summed in bfloat16 or wider, within the bound.
No kernel may reach another device: no remote copies, remote signals or barrier semaphores. Data moves between devices by JAX's collectives and lax.ppermute only.
A program may use at most 128 MiB of HBM per device.

v0:
```python
import jax
import jax.numpy as jnp
from jax import lax
from jax.experimental import pallas as pl
from jax.experimental.pallas import tpu as pltpu
from jax.sharding import PartitionSpec as P

BETA = 1.0
RIDGE = 0.1
AXES = ("gx", "gy", "gz")
ROWS_ROWS = (((1,), (1,)), ((), ()))
VMEM_BYTES = 36 * 2**20
PIVOTS = 8
VOXEL_ROWS = 8
CHUNK = 8
SPLIT = 2
TOGETHER = {"first": 4, "near": 8, "second": 4, "third": 8, "fourth": 4}
f32, bf16 = jnp.float32, jnp.bfloat16


def iota(shape, dim):
    return lax.broadcasted_iota(jnp.int32, shape, dim)


def half_rows(feats, classes):
    return -(-(feats * feats * classes // 128 + feats + 8) // 16) * 8


def moments_of(x, q):
    ny, feats, _ = x.shape
    scatter = first = None
    chunk, part = CHUNK, feats // SPLIT
    for c in range(0, ny, chunk):
        xs = jnp.concatenate([x[y] for y in range(c, c + chunk)], axis=1)
        qs = jnp.concatenate([q[y] for y in range(c, c + chunk)], axis=1)
        ones = jnp.ones((16, xs.shape[1]), bf16)
        s = []
        for g in range(0, feats, part):
            weighted = jnp.concatenate([xs[f : f + 1] * qs for f in range(g, g + part)], axis=0)
            s.append(lax.dot_general(xs, weighted, ROWS_ROWS, preferred_element_type=f32))
        s = jnp.concatenate(s, axis=1)
        m = lax.dot_general(
            jnp.concatenate([xs, ones], axis=0), qs, ROWS_ROWS, preferred_element_type=f32
        )
        scatter = s if scatter is None else scatter + s
        first = m if first is None else first + m
    return scatter, first


def no_moments(feats, classes):
    return jnp.zeros((feats, feats * classes), f32), jnp.zeros((feats + 16, classes), f32)


def put_moments(place_ref, mine, theirs, scatter, first):
    feats, lanes = scatter.shape
    rows = [scatter[:, j : j + 128] for j in range(0, lanes, 128)]
    rows.append(jnp.pad(first[: feats + 8], ((0, 0), (0, 128 - first.shape[1]))))
    half = mine.shape[0]
    rows.append(jnp.zeros((2 * half - sum(r.shape[0] for r in rows), 128), f32))
    rows = jnp.concatenate(rows, axis=0)
    odd = Place(place_ref, 1).sends == 1
    mine[...] = jnp.where(odd, rows[half:], rows[:half])
    theirs[pl.ds(0, half), :] = jnp.where(odd, rows[:half], rows[half:])


def all_moments(place_ref, mine, theirs):
    odd = Place(place_ref, 1).sends == 1
    mine, theirs = mine[...], theirs[...]
    return jnp.concatenate([jnp.where(odd, theirs, mine), jnp.where(odd, mine, theirs)], axis=0)


def m_step(total, w_ref, bias_ref):
    classes = bias_ref.shape[0]
    feats = w_ref.shape[0] // classes
    groups = 128 // classes
    tiles = feats // groups
    lane, sub = iota((8, 128), 1), iota((8, 128), 0)
    group = lane // classes

    def rows(r):
        return total[r : r + 8]

    def spread_lanes(v, g):
        return jnp.take_along_axis(v, lane % classes + g * classes, axis=1, mode="promise_in_bounds")

    def spread_row(v, r):
        return jnp.broadcast_to(v[r : r + 1], (8, 128))

    base = tiles * feats
    counts = spread_lanes(spread_row(rows(base + feats), 0), 0)
    inv = 1.0 / counts
    means = [spread_lanes(rows(base + 8 * j), 0) / counts for j in range(tiles)]
    eye = jnp.where(sub == group, 1.0, 0.0)
    zero = jnp.zeros((8, 128), f32)
    mean_row = [
        jnp.broadcast_to(jnp.sum(eye * m, axis=0, keepdims=True), (8, 128)) for m in means
    ]
    mat = [
        [rows(t * feats + 8 * j) * inv - means[j] * mean_row[t] + (RIDGE * eye if t == j else 0.0) for t in range(tiles)]
        for j in range(tiles)
    ]
    side = [[eye if t == j else zero for t in range(tiles)] for j in range(tiles)] + [mean_row]
    diag = [zero] * tiles
    for p in range(0, feats, PIVOTS):
        at, g0 = p // 8, p % 8
        cols = [("m", j) for j in range(at, tiles)] + [("s", j) for j in (*range(at + 1), tiles)]
        held = {"m": mat, "s": side}
        head = [{(n, j): spread_lanes(held[n][j][at], g0 + s) for n, j in cols} for s in range(PIVOTS)]
        e = [[spread_row(head[s]["m", at], g0 + t) for t in range(PIVOTS)] for s in range(PIVOTS)]
        factors = [
            [spread_row(mat[at][t], g0 + s) if t >= at else None for t in range(tiles)] for s in range(PIVOTS)
        ]
        ells, scaled = {}, []
        for s in range(PIVOTS):
            r = 1.0 / e[s][s]
            for t in range(s + 1, PIVOTS):
                ells[s, t] = e[s][t] * r
                for c in cols:
                    head[t][c] = head[t][c] - ells[s, t] * head[s][c]
                for u in range(t, PIVOTS):
                    e[t][u] = e[t][u] - ells[s, t] * e[s][u]
            scaled.append({c: head[s][c] * r for c in cols})
        for s in reversed(range(PIVOTS)):
            for t in range(s + 1, PIVOTS):
                for c in cols:
                    scaled[s][c] = scaled[s][c] - ells[s, t] * scaled[t][c]
        for t in range(at, tiles):
            for s in range(PIVOTS):
                factor = factors[s][t]
                if t == at:
                    factor = jnp.where(group >= g0 + PIVOTS, factor, 0.0)
                for n, j in cols:
                    held[n][j][t] = held[n][j][t] - factor * scaled[s][n, j]
        for s in range(PIVOTS):
            own = group == g0 + s
            for n, j in cols:
                if n == "s":
                    side[j][at] = jnp.where(own, head[s][n, j], side[j][at])
            diag[at] = jnp.where(own, e[s][s], diag[at])
    logdet = sum(jnp.log(d) for d in diag)
    step = classes
    while step < 128:
        logdet = logdet + pltpu.roll(logdet, step, 1)
        step *= 2
    everything = jnp.sum(counts, axis=1, keepdims=True) * (1.0 / groups)
    bias = jnp.log(counts / everything) - 0.5 * logdet
    for t in range(tiles):
        scale = lax.rsqrt(diag[t])
        shift = -side[tiles][t] * scale
        high = shift.astype(bf16).astype(f32)
        middle = (shift - high).astype(bf16).astype(f32)
        low = shift - high - middle
        parts = jnp.where(sub == 0, high, jnp.where(sub == 1, middle, jnp.where(sub == 2, low, 0.0)))
        block = [side[j][t] * scale for j in range(tiles)] + [parts, zero, bias]
        turned = jnp.concatenate(block + [zero] * (16 - len(block)), axis=0).T
        w_ref[pl.ds(t * 128, 128), :] = turned[:, : feats + 16].astype(bf16)
        if t == 0:
            bias_ref[...] = jnp.broadcast_to(turned[:classes, feats + 16 : feats + 17], (classes, 128))
    return means


def loglik_of(x, w_ref, bias):
    parts = [loglik_part(x[j : j + VOXEL_ROWS], w_ref, bias) for j in range(0, x.shape[0], VOXEL_ROWS)]
    return jnp.concatenate(parts, axis=0)


def loglik_part(x, w_ref, bias):
    n, feats, nz = x.shape
    classes = bias.shape[0]
    xs = jnp.concatenate([x[j] for j in range(n)], axis=1)
    xs = jnp.concatenate([xs, jnp.ones((16, n * nz), bf16)], axis=0)
    white = jnp.dot(w_ref[...], xs, preferred_element_type=f32)
    white = white * white
    square = white[:classes]
    for g in range(1, feats):
        square = square + white[g * classes : (g + 1) * classes]
    return jnp.stack(
        [bias[:, :nz] - 0.5 * square[:, j * nz : (j + 1) * nz] for j in range(n)], axis=0
    )


def sharing(ny):
    return 128 // (2 * ny)


def own_lane(i, nx, ny, classes):
    start = 2 * ny * (i // (nx // sharing(ny)))
    lane, y = iota((ny, classes, 128), 2), iota((ny, classes, 128), 0)
    return (lane == start + y) | (lane == start + ny + y)


def shift_matrix(ny, nz):
    src, dst = iota((nz + 128, nz), 0), iota((nz + 128, nz), 1)
    near = (src < nz) & ((src == dst + 1) | (src == dst - 1))
    face = src - nz
    first = face % (2 * ny) < ny
    edge = (face >= 0) & ((first & (dst == nz - 1)) | (jnp.logical_not(first) & (dst == 0)))
    return jnp.where(near | edge, 1.0, 0.0).astype(bf16)


def take_matrix(ny, nz):
    src, dst = iota((nz, 128), 0), iota((nz, 128), 1)
    first = dst % (2 * ny) < ny
    hit = ((src == 0) & first) | ((src == nz - 1) & jnp.logical_not(first))
    return jnp.where(hit, 1.0, 0.0).astype(bf16)


def near_of(i, q_ref, y_halo, z_halo):
    nx, ny, classes, nz = q_ref.shape
    nx = nx - 2
    mid = q_ref[i + 1]
    down = q_ref[i].astype(f32)
    up = q_ref[i + 2].astype(f32)
    mid32 = mid.astype(f32)
    left = jnp.concatenate([y_halo[0, pl.ds(i, 1)], mid32[:-1]], axis=0)
    right = jnp.concatenate([mid32[1:], y_halo[1, pl.ds(i, 1)]], axis=0)
    face = z_halo[i % (nx // sharing(ny))]
    face = jnp.where(own_lane(i, nx, ny, classes), face[None], 0.0).astype(bf16)
    both = jnp.concatenate([mid, face], axis=2).reshape(ny * classes, nz + 128)
    along = jnp.dot(both, shift_matrix(ny, nz), preferred_element_type=f32)
    return (down + up) + (left + right) + along.reshape(ny, classes, nz)


def update_of(scores, near):
    s = scores + BETA * near
    e = jnp.exp(s - jnp.max(s, axis=1, keepdims=True))
    return (e * (1.0 / jnp.sum(e, axis=1, keepdims=True))).astype(bf16)


class Place:
    def __init__(self, place_ref, axis):
        self.sends, self.gets, self.before, self.after = (place_ref[4 * axis + j] for j in range(4))

    def halo(self, inner, outer):
        before = jnp.where(self.gets == 1, inner, outer)
        after = jnp.where(self.gets == 1, outer, inner)
        before = jnp.where(self.before == 1, before, 0.0)
        after = jnp.where(self.after == 1, after, 0.0)
        return before, after


def fill_halo(place_ref, halo, q_ref, padded, y_halo, z_halo):
    xi, xo, yi, yo, zi, zo = halo
    nx, ny, classes, nz = q_ref.shape
    before, after = Place(place_ref, 0).halo(xi[...].astype(f32), xo[...].astype(f32))
    padded[0], padded[nx + 1] = before.astype(bf16), after.astype(bf16)
    for i in range(nx):
        padded[i + 1] = q_ref[i]
    rows = y_halo.shape[1] * classes
    before, after = Place(place_ref, 1).halo(*(y[pl.ds(y.shape[0] - rows, rows), :] for y in (yi, yo)))
    y_halo[0], y_halo[1] = before.reshape(y_halo.shape[1:]), after.reshape(y_halo.shape[1:])
    rows = z_halo.shape[0] * classes
    before, after = Place(place_ref, 2).halo(*(z[pl.ds(z.shape[0] - rows, rows), :] for z in (zi, zo)))
    first = iota(before.shape, 1) % (2 * ny) < ny
    z_halo[...] = jnp.where(first, after, before).reshape(z_halo.shape)


def put_faces(place_ref, brick, xin, xout, yin, yout, zface):
    nx, ny, classes, nz = brick.shape
    first_in, first_in_y = Place(place_ref, 0).sends == 1, Place(place_ref, 1).sends == 1
    xin[...] = jnp.where(first_in, brick[0], brick[nx - 1])
    xout[...] = jnp.where(first_in, brick[nx - 1], brick[0])
    first = jnp.concatenate([brick[i, 0] for i in range(nx)], axis=0).astype(f32)
    last = jnp.concatenate([brick[i, ny - 1] for i in range(nx)], axis=0).astype(f32)
    rows = nx * classes
    yin[pl.ds(yin.shape[0] - rows, rows), :] = jnp.where(first_in_y, first, last)
    yout[...] = jnp.where(first_in_y, last, first)
    share = nx // sharing(ny)
    for j in range(share):
        total = None
        for i in range(j, nx, share):
            spread = jnp.dot(brick[i].reshape(ny * classes, nz), take_matrix(ny, nz), preferred_element_type=f32)
            spread = jnp.where(own_lane(i, nx, ny, classes), spread.reshape(ny, classes, 128), 0.0)
            spread = jnp.sum(spread, axis=0)
            total = spread if total is None else total + spread
        zface[pl.ds(j * classes, classes), :] = total


def over_slabs(nx, together, body, carry=None):
    def step(j, carry):
        for i in range(together):
            carry = body(j * together + i, carry)
        return carry

    if together == nx:
        return step(0, carry)
    return lax.fori_loop(0, nx // together, step, carry)


def all_near(near, space):
    def body(i, carry):
        near[i] = near_of(i, *space)
        return carry

    over_slabs(near.shape[0], TOGETHER["near"], body, 0)


def first_kernel(place, x_hbm, q_hbm, xt, qt, xin, xout, yout, zface, mine, theirs, x_in, q_in, sems):
    nx = xt.shape[0]
    feats, classes = xt.shape[2], qt.shape[2]

    def copies(i):
        return (
            pltpu.make_async_copy(q_hbm.at[:, i], q_in.at[i], sems.at[0, i]),
            pltpu.make_async_copy(x_hbm.at[:, i], x_in.at[i], sems.at[1, i]),
        )

    for i in range(nx):
        for copy in copies(i):
            copy.start()

    def slab(i, sums):
        for copy in copies(i):
            copy.wait()
        x = jnp.swapaxes(x_in[i], 0, 1)
        q = jnp.swapaxes(q_in[i], 0, 1)
        xt[i], qt[i] = x, q
        return jax.tree.map(jnp.add, sums, moments_of(x, q))

    sums = over_slabs(nx, TOGETHER["first"], slab, no_moments(feats, classes))
    put_faces(place, qt, xin, xout, theirs, yout, zface)
    put_moments(place, mine, theirs, *sums)


def second_kernel(
    place, mine, theirs, xt, qt, xi, xo, yi, yo, zi, zo, sc, q1, xin, xout, yin, yout, zface, w, bias, near, *space
):
    nx = xt.shape[0]
    fill_halo(place, (xi, xo, yi, yo, zi, zo), qt, *space)
    all_near(near, space)
    m_step(all_moments(place, mine, theirs), w, bias)

    def slab(i, carry):
        scores = loglik_of(xt[i], w, bias[...])
        sc[i] = scores
        q1[i] = update_of(scores, near[i])
        return carry

    over_slabs(nx, TOGETHER["second"], slab, 0)
    put_faces(place, q1, xin, xout, yin, yout, zface)


def third_kernel(place, sc, xt, qt, xi, xo, yi, yo, zi, zo, q2, xin, xout, yout, zface, mine, theirs, *space):
    nx = xt.shape[0]
    fill_halo(place, (xi, xo, yi, yo, zi, zo), qt, *space)

    def slab(i, sums):
        q = update_of(sc[i], near_of(i, *space))
        q2[i] = q
        return jax.tree.map(jnp.add, sums, moments_of(xt[i], q))

    sums = over_slabs(nx, TOGETHER["third"], slab, no_moments(xt.shape[2], qt.shape[2]))
    put_faces(place, q2, xin, xout, theirs, yout, zface)
    put_moments(place, mine, theirs, *sums)


def fourth_kernel(place, mine, theirs, xt, qt, xi, xo, yi, yo, zi, zo, seg, means_ref, w, bias, near, *space):
    nx = xt.shape[0]
    classes, feats = means_ref.shape
    fill_halo(place, (xi, xo, yi, yo, zi, zo), qt, *space)
    all_near(near, space)
    means = jnp.concatenate(m_step(all_moments(place, mine, theirs), w, bias), axis=0)
    means = jnp.concatenate([means, jnp.zeros((128 - feats, 128), f32)], axis=0).T
    means_ref[...] = means[:classes, :feats]

    def slab(i, carry):
        q = update_of(loglik_of(xt[i], w, bias[...]), near[i])
        seg[:, i] = jnp.swapaxes(q, 0, 1)
        return carry

    over_slabs(nx, TOGETHER["fourth"], slab, 0)


def pairings(n):
    if n == 2:
        return [[1, 0]]
    if n == 4:
        return [[1, 0, 3, 2], [3, 2, 1, 0], [2, 3, 0, 1]]
    return None


def send(value, axis, to):
    return lax.ppermute(value, axis, list(enumerate(to)))


def place_along(axis):
    n, at = lax.axis_size(axis), lax.axis_index(axis)
    if pairings(n) is None:
        return [0 * at, 0 * at + 1, at > 0, at < n - 1]
    return [at % 2, at % 2, at > 0, at < n - 1]


def send_middle(value, axis, other):
    n = lax.axis_size(other)
    if n % 2:
        return send(value, axis, pairings(4)[1])
    pairs = []
    for a in range(4):
        for o in range(n):
            here, there = (a, o), (3 - a, o) if a in (1, 2) else (a, o ^ 1)
            if axis == "gx":
                pairs.append((here[0] * n + here[1], there[0] * n + there[1]))
            else:
                pairs.append((here[1] * 4 + here[0], there[1] * 4 + there[0]))
    return lax.ppermute(value, ("gx", "gz"), pairs)


def swap(axis, inner, outer):
    n = lax.axis_size(axis)
    if n == 2:
        got = send(inner, axis, [1, 0])
        return got, got
    if n == 4:
        return send(inner, axis, pairings(n)[0]), send_middle(outer, axis, "gz" if axis == "gx" else "gx")
    return send(inner, axis, [(i + 1) % n for i in range(n)]), send(outer, axis, [(i - 1) % n for i in range(n)])


def exchange(xin, xout, yin, yout, zface):
    return *swap("gx", xin, xout), *swap("gy", yin, yout), *swap("gz", zface, zface)


def sum_and_exchange(xin, xout, yout, zface, mine, theirs):
    rows = mine.shape[0]
    paired = lax.axis_size("gy") == 2
    if paired:
        yi = yo = send(theirs, "gy", [1, 0])
        total = mine + yi[:rows]
    else:
        yi, yo = swap("gy", theirs[rows:], yout)
        total = lax.psum(jnp.concatenate([mine, theirs[:rows]], axis=0), "gy")
    if lax.axis_size("gx") == 4:
        total = sum((send(total, "gx", to) for to in pairings(4)), total)
    else:
        total = lax.psum(total, "gx")
    total, xin, xout = lax.optimization_barrier((total, xin, xout))
    xi, xo = swap("gx", xin, xout)
    if lax.axis_size("gz") == 4:
        n = total.shape[0]
        both = jnp.concatenate([total, zface], axis=0)
        zi, zo = (send(both, "gz", to) for to in pairings(4)[:2])
        total = total + zi[:n] + zo[:n] + send(total, "gz", pairings(4)[2])
    else:
        zi, zo = swap("gz", zface, zface)
        total = lax.psum(total, "gz")
    halves = (total, send(total, "gy", [1, 0])) if paired else (total[:rows], total[rows:])
    return *halves, xi, xo, yi, yo, zi, zo


def call(kernel, outs, scratch, places, *args, vmem=VMEM_BYTES):
    specs = [pl.BlockSpec(memory_space=place) for place in places]
    specs += [pl.BlockSpec(memory_space=pltpu.VMEM)] * (len(args) - len(places))
    return pl.pallas_call(
        kernel,
        out_shape=tuple(outs),
        in_specs=specs,
        out_specs=tuple(pl.BlockSpec(memory_space=pltpu.VMEM) for _ in outs),
        scratch_shapes=scratch,
        compiler_params=pltpu.CompilerParams(vmem_limit_bytes=vmem),
    )(*args)


class Sizes:
    def __init__(self, feats, classes, nx, ny, nz):
        shape = jax.ShapeDtypeStruct
        half = half_rows(feats, classes)
        share = nx // sharing(ny)
        self.features = shape((nx, ny, feats, nz), bf16)
        self.scores = shape((nx, ny, classes, nz), f32)
        self.brick = shape((nx, ny, classes, nz), bf16)
        self.face_x = shape((ny, classes, nz), bf16)
        self.face_y = shape((nx * classes, nz), f32)
        self.face_z = shape((share * classes, 128), f32)
        self.mine = shape((half, 128), f32)
        self.theirs = shape((half + nx * classes, 128), f32)
        self.out = shape((classes, nx, ny, nz), bf16)
        self.means = shape((classes, feats), f32)
        self.solved = [
            pltpu.VMEM((feats * classes, feats + 16), bf16),
            pltpu.VMEM((classes, 128), f32),
            pltpu.VMEM((nx, ny, classes, nz), f32),
        ]
        self.halos = [
            pltpu.VMEM((nx + 2, ny, classes, nz), bf16),
            pltpu.VMEM((2, nx, classes, nz), f32),
            pltpu.VMEM((share, classes, 128), f32),
        ]
        self.arrived = [
            pltpu.VMEM((nx, feats, ny, nz), bf16),
            pltpu.VMEM((nx, classes, ny, nz), bf16),
            pltpu.SemaphoreType.DMA((2, nx)),
        ]


def run_first(z, place, features, posteriors):
    outs = [z.features, z.brick, z.face_x, z.face_x, z.face_y, z.face_z, z.mine, z.theirs]
    places = [pltpu.SMEM, pltpu.HBM, pltpu.HBM]
    return call(first_kernel, outs, z.arrived, places, place, features, posteriors, vmem=48 * 2**20)


def run_second(z, place, mine, theirs, xt, qt, *halo):
    outs = [z.scores, z.brick, z.face_x, z.face_x, z.face_y, z.face_y, z.face_z]
    return call(second_kernel, outs, z.solved + z.halos, [pltpu.SMEM], place, mine, theirs, xt, qt, *halo)


def run_third(z, place, sc, xt, qt, *halo):
    outs = [z.brick, z.face_x, z.face_x, z.face_y, z.face_z, z.mine, z.theirs]
    return call(third_kernel, outs, z.halos, [pltpu.SMEM], place, sc, xt, qt, *halo)


def run_fourth(z, place, mine, theirs, xt, qt, *halo):
    return call(
        fourth_kernel, [z.out, z.means], z.solved + z.halos, [pltpu.SMEM], place, mine, theirs, xt, qt, *halo
    )


def local(features, posteriors):
    feats, nx, ny, nz = features.shape
    z = Sizes(feats, posteriors.shape[0], nx, ny, nz)
    place = jnp.stack([jnp.asarray(v, jnp.int32) for axis in AXES for v in place_along(axis)])
    xt, qt, *edge = run_first(z, place, features, posteriors)
    mine, theirs, *halo = sum_and_exchange(*edge)
    sc, q1, *edge = run_second(z, place, mine, theirs, xt, qt, *halo)
    halo = exchange(*edge)
    q2, *edge = run_third(z, place, sc, xt, q1, *halo)
    mine, theirs, *halo = sum_and_exchange(*edge)
    return run_fourth(z, place, mine, theirs, xt, q2, *halo)


def solution(mesh):
    placed = P(None, "gx", "gy", "gz")
    return jax.shard_map(
        local, mesh=mesh, in_specs=(placed, placed), out_specs=(placed, P()), check_vma=False
    )
```

profile of v0, /device:TPU:0, one launch (start us, length us, event | category | flops | bytes accessed | tf_op | source)
XLA Modules:
  0.0 102.5 jit_solution(9534697749531018058)
XLA Ops:
  0.7 0.1 stack.66.place
  0.8 0.0 copy-start
  0.8 1.2 %copy-done = bf16[16,8,32,128]{3,2,1,0:T(8,128)(2,1)S(1)} copy-done((bf16[16,8,32,128]{3,2,1,0:T(8,128)(2,1)S(1)}, bf16[16,8,32,128]{3,2,1,0:T(8,128)(2,1)}, u32[]{:S(2)}) %copy-start) | copy-done | bytes 1048600
  2.0 13.9 %shard_map.41 = (bf16[8,32,32,128]{3,2,1,0:T(8,128)(2,1)S(1)}, bf16[8,32,16,128]{3,2,1,0:T(8,128)(2,1)S(1)}, bf16[32,16,128]{2,1,0:T(8,128)(2,1)S(1)}, bf16[32,1...) custom-call(s32[12]{0:T(128)S(1)} %stack.66.place, ...), custom_call_target="tpu_custom_call" | custom-call | tf_op jit(solution)/shard_map/pallas_call | solution.py:452
  15.9 0.5 collective-permute-start
  16.5 1.0 collective-permute-done.yi.yo
  17.4 2.9 %collective-permute-start.3 = (f32[88,128]{1,0:T(8,128)S(1)}, f32[88,128]{1,0:T(8,128)S(1)}, u32[]{:S(2)}, u32[]{:S(2)}) collective-permute-start(f32[88,128]{1,0:T(8,128)S(1)} %slice_add_fusion.5), channel_id=1, source_target_pairs={{0,16},{8,24},{16,0},{24,8},{1,17},{9,25},{17,1},{25,9},{2,18},{10... | collective-permute-start | bytes 135176 | tf_op jit(solution)/shard_map/ppermute | solution.py:383
  20.4 1.4 %collective-permute-start.2 = (f32[88,128]{1,0:T(8,128)S(1)}, f32[88,128]{1,0:T(8,128)S(1)}, u32[]{:S(2)}, u32[]{:S(2)}) collective-permute-start(f32[88,128]{1,0:T(8,128)S(1)} %slice_add_fusion.5), channel_id=1, source_target_pairs={{0,24},{8,16},{16,8},{24,0},{1,25},{9,17},{17,9},{25,1},{2,26},{10... | collective-permute-start | bytes 135176 | tf_op jit(solution)/shard_map/ppermute | solution.py:383
  21.8 0.1 collective-permute-start.1
  21.9 0.5 collective-permute-done.3
  22.4 3.3 %collective-permute-done.2 = f32[88,128]{1,0:T(8,128)S(1)} collective-permute-done((f32[88,128]{1,0:T(8,128)S(1)}, f32[88,128]{1,0:T(8,128)S(1)}, u32[]{:S(2)}, u32[]{:S(2)}) %collective-permute-start.2) | collective-permute-done | bytes 45088 | tf_op jit(solution)/shard_map/ppermute | solution.py:383
  25.7 0.1 collective-permute-done.1
  25.9 3.7 %collective-permute-start.5 = (f32[152,128]{1,0:T(8,128)S(1)}, f32[152,128]{1,0:T(8,128)S(1)}, u32[]{:S(2)}, u32[]{:S(2)}) collective-permute-start(f32[152,128]{1,0:T(8,128)S(1)} %constant_dynamic-update-slice_fusion), channel_id=1, source_target_pairs={{0,3},{1,2},{2,1},{3,0},{4,7},{5,6},{6,5},{7,4},{8,11},{9,10},{10,... | collective-permute-start | bytes 233480 | tf_op jit(solution)/shard_map/ppermute | solution.py:383
  29.6 0.0 collective-permute-start.4
  29.6 0.8 collective-permute-start.6
  30.3 1.0 collective-permute-start.8
  31.3 1.2 %collective-permute-start.9 = (bf16[32,16,128]{2,1,0:T(8,128)(2,1)S(1)}, bf16[32,16,128]{2,1,0:T(8,128)(2,1)S(1)}, u32[]{:S(2)}, u32[]{:S(2)}) collective-permute-start(bf16[32,16,128]{2,1,0:T(8,128)(2,1)S(1)} %get-tuple-element.36), channel_id=1, source_target_pairs={{0,1},{1,0},{2,3},{3,2},{8,16},{9,17},{10,18},{11,19},{16,8},{17,9... | collective-permute-start | bytes 393224 | tf_op jit(solution)/shard_map/ppermute | solution.py:405
  32.5 2.1 %collective-permute-done.6 = f32[88,128]{1,0:T(8,128)S(1)} collective-permute-done((f32[88,128]{1,0:T(8,128)S(1)}, f32[88,128]{1,0:T(8,128)S(1)}, u32[]{:S(2)}, u32[]{:S(2)}) %collective-permute-start.6) | collective-permute-done | bytes 45088 | tf_op jit(solution)/shard_map/ppermute | solution.py:383
  34.6 0.0 collective-permute-done.5.zo
  34.6 0.7 collective-permute-done.4.zi
  35.3 0.1 collective-permute-start.7
  35.4 1.2 %collective-permute-done.7.theirs = f32[88,128]{1,0:T(8,128)S(1)} collective-permute-done((f32[88,128]{1,0:T(8,128)S(1)}, f32[88,128]{1,0:T(8,128)S(1)}, u32[]{:S(2)}, u32[]{:S(2)}) %collective-permute-start.7) | collective-permute-done | bytes 45088 | tf_op jit(solution)/shard_map/ppermute | solution.py:383
  36.6 0.0 collective-permute-done.8.xi
  36.6 0.6 collective-permute-done.9.xo
  37.2 12.8 %shard_map.42 = (f32[8,32,16,128]{3,2,1,0:T(8,128)S(1)}, bf16[8,32,16,128]{3,2,1,0:T(8,128)(2,1)S(1)}, bf16[32,16,128]{2,1,0:T(8,128)(2,1)S(1)}, bf16[32,16,128]...) custom-call(s32[12]{0:T(128)S(1)} %stack.66.place, ...), custom_call_target="tpu_custom_call" | custom-call | tf_op jit(solution)/shard_map/pallas_call | solution.py:452
  50.0 1.0 collective-permute-start.10
  51.0 1.3 %collective-permute-start.11 = (bf16[32,16,128]{2,1,0:T(8,128)(2,1)S(1)}, bf16[32,16,128]{2,1,0:T(8,128)(2,1)S(1)}, u32[]{:S(2)}, u32[]{:S(2)}) collective-permute-start(bf16[32,16,128]{2,1,0:T(8,128)(2,1)S(1)} %get-tuple-element.40), channel_id=1, source_target_pairs={{0,1},{1,0},{2,3},{3,2},{8,16},{9,17},{10,18},{11,19},{16,8},{17,9... | collective-permute-start | bytes 393224 | tf_op jit(solution)/shard_map/ppermute | solution.py:405
  52.3 0.0 collective-permute-start.12
  52.3 0.7 collective-permute-start.14
  53.1 2.6 %collective-permute-start.13 = (f32[64,128]{1,0:T(8,128)S(1)}, f32[64,128]{1,0:T(8,128)S(1)}, u32[]{:S(2)}, u32[]{:S(2)}) collective-permute-start(f32[64,128]{1,0:T(8,128)S(1)} %get-tuple-element.42), channel_id=1, source_target_pairs={{0,1},{1,0},{2,3},{3,2},{4,5},{5,4},{6,7},{7,6},{8,9},{9,8},{10,11... | collective-permute-start | bytes 98312 | tf_op jit(solution)/shard_map/ppermute | solution.py:383
  55.7 2.8 %collective-permute-done.14.zo = f32[64,128]{1,0:T(8,128)S(1)} collective-permute-done((f32[64,128]{1,0:T(8,128)S(1)}, f32[64,128]{1,0:T(8,128)S(1)}, u32[]{:S(2)}, u32[]{:S(2)}) %collective-permute-start.14) | collective-permute-done | bytes 32800 | tf_op jit(solution)/shard_map/ppermute | solution.py:405
  58.5 0.0 collective-permute-done.13.zi
  58.5 0.0 collective-permute-done.12.yi.yo
  58.5 0.0 collective-permute-done.10.xi
  58.5 0.0 collective-permute-done.11.xo
  58.5 12.8 %shard_map.43 = (bf16[8,32,16,128]{3,2,1,0:T(8,128)(2,1)S(1)}, bf16[32,16,128]{2,1,0:T(8,128)(2,1)S(1)}, bf16[32,16,128]{2,1,0:T(8,128)(2,1)S(1)}, f32[128,128]{...) custom-call(s32[12]{0:T(128)S(1)} %stack.66.place, ...), custom_call_target="tpu_custom_call" | custom-call | tf_op jit(solution)/shard_map/pallas_call | solution.py:452
  71.2 0.0 collective-permute-start.15
  71.2 1.3 %collective-permute-done.15.yi.yo = f32[216,128]{1,0:T(8,128)S(1)} collective-permute-done((f32[216,128]{1,0:T(8,128)S(1)}, f32[216,128]{1,0:T(8,128)S(1)}, u32[]{:S(2)}, u32[]{:S(2)}) %collective-permute-start.15) | collective-permute-done | bytes 110624 | tf_op jit(solution)/shard_map/ppermute | solution.py:383
  72.6 1.1 %collective-permute-start.18 = (f32[88,128]{1,0:T(8,128)S(1)}, f32[88,128]{1,0:T(8,128)S(1)}, u32[]{:S(2)}, u32[]{:S(2)}) collective-permute-start(f32[88,128]{1,0:T(8,128)S(1)} %slice_add_fusion.2), channel_id=1, source_target_pairs={{0,16},{8,24},{16,0},{24,8},{1,17},{9,25},{17,1},{25,9},{2,18},{10... | collective-permute-start | bytes 135176 | tf_op jit(solution)/shard_map/ppermute | solution.py:383
  73.7 1.4 %collective-permute-start.17 = (f32[88,128]{1,0:T(8,128)S(1)}, f32[88,128]{1,0:T(8,128)S(1)}, u32[]{:S(2)}, u32[]{:S(2)}) collective-permute-start(f32[88,128]{1,0:T(8,128)S(1)} %slice_add_fusion.2), channel_id=1, source_target_pairs={{0,24},{8,16},{16,8},{24,0},{1,25},{9,17},{17,9},{25,1},{2,26},{10... | collective-permute-start | bytes 135176 | tf_op jit(solution)/shard_map/ppermute | solution.py:383
  75.1 1.0 %collective-permute-start.16 = (f32[88,128]{1,0:T(8,128)S(1)}, f32[88,128]{1,0:T(8,128)S(1)}, u32[]{:S(2)}, u32[]{:S(2)}) collective-permute-start(f32[88,128]{1,0:T(8,128)S(1)} %slice_add_fusion.2), channel_id=1, source_target_pairs={{0,8},{8,0},{16,24},{24,16},{1,9},{9,1},{17,25},{25,17},{2,10},{10... | collective-permute-start | bytes 135176 | tf_op jit(solution)/shard_map/ppermute | solution.py:383
  76.1 0.6 collective-permute-done.18
  76.7 2.0 %collective-permute-done.17 = f32[88,128]{1,0:T(8,128)S(1)} collective-permute-done((f32[88,128]{1,0:T(8,128)S(1)}, f32[88,128]{1,0:T(8,128)S(1)}, u32[]{:S(2)}, u32[]{:S(2)}) %collective-permute-start.17) | collective-permute-done | bytes 45088 | tf_op jit(solution)/shard_map/ppermute | solution.py:383
  78.7 0.5 collective-permute-done.16
  79.2 1.9 %collective-permute-start.20 = (f32[152,128]{1,0:T(8,128)S(1)}, f32[152,128]{1,0:T(8,128)S(1)}, u32[]{:S(2)}, u32[]{:S(2)}) collective-permute-start(f32[152,128]{1,0:T(8,128)S(1)} %constant_dynamic-update-slice_fusion.2), channel_id=1, source_target_pairs={{0,3},{1,2},{2,1},{3,0},{4,7},{5,6},{6,5},{7,4},{8,11},{9,10},{10,... | collective-permute-start | bytes 233480 | tf_op jit(solution)/shard_map/ppermute | solution.py:383
  81.1 0.7 collective-permute-start.19
  81.8 1.8 %collective-permute-start.21 = (f32[88,128]{1,0:T(8,128)S(1)}, f32[88,128]{1,0:T(8,128)S(1)}, u32[]{:S(2)}, u32[]{:S(2)}) collective-permute-start(f32[88,128]{1,0:T(8,128)S(1)} %add_add_fusion), channel_id=1, source_target_pairs={{0,2},{1,3},{2,0},{3,1},{4,6},{5,7},{6,4},{7,5},{8,10},{9,11},{10,... | collective-permute-start | bytes 135176 | tf_op jit(solution)/shard_map/ppermute | solution.py:383
  83.6 1.0 %collective-permute-start.23 = (bf16[32,16,128]{2,1,0:T(8,128)(2,1)S(1)}, bf16[32,16,128]{2,1,0:T(8,128)(2,1)S(1)}, u32[]{:S(2)}, u32[]{:S(2)}) collective-permute-start(bf16[32,16,128]{2,1,0:T(8,128)(2,1)S(1)} %get-tuple-element.50), channel_id=1, source_target_pairs={{0,8},{8,0},{16,24},{24,16},{1,9},{9,1},{17,25},{25,17},{2,10},{10... | collective-permute-start | bytes 393224 | tf_op jit(solution)/shard_map/ppermute | solution.py:383
  84.7 0.3 collective-permute-start.24
  84.9 1.9 %collective-permute-done.21 = f32[88,128]{1,0:T(8,128)S(1)} collective-permute-done((f32[88,128]{1,0:T(8,128)S(1)}, f32[88,128]{1,0:T(8,128)S(1)}, u32[]{:S(2)}, u32[]{:S(2)}) %collective-permute-start.21) | collective-permute-done | bytes 45088 | tf_op jit(solution)/shard_map/ppermute | solution.py:383
  86.9 0.0 collective-permute-done.20.zo
  86.9 0.8 collective-permute-done.19.zi
  87.7 0.1 collective-permute-start.22
  87.8 1.2 %collective-permute-done.22.theirs = f32[88,128]{1,0:T(8,128)S(1)} collective-permute-done((f32[88,128]{1,0:T(8,128)S(1)}, f32[88,128]{1,0:T(8,128)S(1)}, u32[]{:S(2)}, u32[]{:S(2)}) %collective-permute-start.22) | collective-permute-done | bytes 45088 | tf_op jit(solution)/shard_map/ppermute | solution.py:383
  89.0 0.0 collective-permute-done.23.xi
  89.0 0.7 collective-permute-done.24.xo
  89.7 12.8 %shard_map.44 = (bf16[16,8,32,128]{3,2,1,0:T(8,128)(2,1)}, f32[16,32]{1,0:T(8,128)}) custom-call(s32[12]{0:T(128)S(1)} %stack.66.place, f32[88,128]{1,0:T(8,128)S(1)} %fusion.mine, f32[88,128]{1,0:T(8,128)S(1)} %collective-permute-done.22.theirs, bf16[8,32,32,128]{3,2,1,0:T(8,128)(2,1)S(1)} %get-tuple-element.33.xt, ...), custom_call_target="tpu_custom_call" | custom-call | tf_op jit(solution)/shard_map/pallas_call | solution.py:452
  (10 shorter events, 0.1 us)
Async XLA Ops:
  0.8 1.2 %copy-start = (bf16[16,8,32,128]{3,2,1,0:T(8,128)(2,1)S(1)}, bf16[16,8,32,128]{3,2,1,0:T(8,128)(2,1)}, u32[]{:S(2)}) copy-start(bf16[16,8,32,128]{3,2,1,0:T(8,128)(2,1)} %q_hbm.1) | copy-start | bytes 3145732
  15.9 1.5 %collective-permute-start = (f32[216,128]{1,0:T(8,128)S(1)}, f32[216,128]{1,0:T(8,128)S(1)}, u32[]{:S(2)}, u32[]{:S(2)}) collective-permute-start(f32[216,128]{1,0:T(8,128)S(1)} %get-tuple-element.28), channel_id=1, source_target_pairs={{0,4},{4,0},{1,5},{5,1},{2,6},{6,2},{3,7},{7,3},{8,12},{12,8},{9,1... | collective-permute-start | bytes 331784 | tf_op jit(solution)/shard_map/ppermute | solution.py:383
  17.4 5.0 %collective-permute-start.3 = (f32[88,128]{1,0:T(8,128)S(1)}, f32[88,128]{1,0:T(8,128)S(1)}, u32[]{:S(2)}, u32[]{:S(2)}) collective-permute-start(f32[88,128]{1,0:T(8,128)S(1)} %slice_add_fusion.5), channel_id=1, source_target_pairs={{0,16},{8,24},{16,0},{24,8},{1,17},{9,25},{17,1},{25,9},{2,18},{10... | collective-permute-start | bytes 135176 | tf_op jit(solution)/shard_map/ppermute | solution.py:383
  20.4 5.4 %collective-permute-start.2 = (f32[88,128]{1,0:T(8,128)S(1)}, f32[88,128]{1,0:T(8,128)S(1)}, u32[]{:S(2)}, u32[]{:S(2)}) collective-permute-start(f32[88,128]{1,0:T(8,128)S(1)} %slice_add_fusion.5), channel_id=1, source_target_pairs={{0,24},{8,16},{16,8},{24,0},{1,25},{9,17},{17,9},{25,1},{2,26},{10... | collective-permute-start | bytes 135176 | tf_op jit(solution)/shard_map/ppermute | solution.py:383
  21.8 4.0 %collective-permute-start.1 = (f32[88,128]{1,0:T(8,128)S(1)}, f32[88,128]{1,0:T(8,128)S(1)}, u32[]{:S(2)}, u32[]{:S(2)}) collective-permute-start(f32[88,128]{1,0:T(8,128)S(1)} %slice_add_fusion.5), channel_id=1, source_target_pairs={{0,8},{8,0},{16,24},{24,16},{1,9},{9,1},{17,25},{25,17},{2,10},{10... | collective-permute-start | bytes 135176 | tf_op jit(solution)/shard_map/ppermute | solution.py:383
  25.9 8.7 %collective-permute-start.5 = (f32[152,128]{1,0:T(8,128)S(1)}, f32[152,128]{1,0:T(8,128)S(1)}, u32[]{:S(2)}, u32[]{:S(2)}) collective-permute-start(f32[152,128]{1,0:T(8,128)S(1)} %constant_dynamic-update-slice_fusion), channel_id=1, source_target_pairs={{0,3},{1,2},{2,1},{3,0},{4,7},{5,6},{6,5},{7,4},{8,11},{9,10},{10,... | collective-permute-start | bytes 233480 | tf_op jit(solution)/shard_map/ppermute | solution.py:383
  29.6 5.8 %collective-permute-start.4 = (f32[152,128]{1,0:T(8,128)S(1)}, f32[152,128]{1,0:T(8,128)S(1)}, u32[]{:S(2)}, u32[]{:S(2)}) collective-permute-start(f32[152,128]{1,0:T(8,128)S(1)} %constant_dynamic-update-slice_fusion), channel_id=1, source_target_pairs={{0,1},{1,0},{2,3},{3,2},{4,5},{5,4},{6,7},{7,6},{8,9},{9,8},{10,11... | collective-permute-start | bytes 233480 | tf_op jit(solution)/shard_map/ppermute | solution.py:383
  29.6 5.1 %collective-permute-start.6 = (f32[88,128]{1,0:T(8,128)S(1)}, f32[88,128]{1,0:T(8,128)S(1)}, u32[]{:S(2)}, u32[]{:S(2)}) collective-permute-start(f32[88,128]{1,0:T(8,128)S(1)} %add_add_fusion.1), channel_id=1, source_target_pairs={{0,2},{1,3},{2,0},{3,1},{4,6},{5,7},{6,4},{7,5},{8,10},{9,11},{10,... | collective-permute-start | bytes 135176 | tf_op jit(solution)/shard_map/ppermute | solution.py:383
  30.3 6.3 %collective-permute-start.8 = (bf16[32,16,128]{2,1,0:T(8,128)(2,1)S(1)}, bf16[32,16,128]{2,1,0:T(8,128)(2,1)S(1)}, u32[]{:S(2)}, u32[]{:S(2)}) collective-permute-start(bf16[32,16,128]{2,1,0:T(8,128)(2,1)S(1)} %get-tuple-element.35), channel_id=1, source_target_pairs={{0,8},{8,0},{16,24},{24,16},{1,9},{9,1},{17,25},{25,17},{2,10},{10... | collective-permute-start | bytes 393224 | tf_op jit(solution)/shard_map/ppermute | solution.py:383
  31.3 5.9 %collective-permute-start.9 = (bf16[32,16,128]{2,1,0:T(8,128)(2,1)S(1)}, bf16[32,16,128]{2,1,0:T(8,128)(2,1)S(1)}, u32[]{:S(2)}, u32[]{:S(2)}) collective-permute-start(bf16[32,16,128]{2,1,0:T(8,128)(2,1)S(1)} %get-tuple-element.36), channel_id=1, source_target_pairs={{0,1},{1,0},{2,3},{3,2},{8,16},{9,17},{10,18},{11,19},{16,8},{17,9... | collective-permute-start | bytes 393224 | tf_op jit(solution)/shard_map/ppermute | solution.py:405
  35.3 1.3 %collective-permute-start.7 = (f32[88,128]{1,0:T(8,128)S(1)}, f32[88,128]{1,0:T(8,128)S(1)}, u32[]{:S(2)}, u32[]{:S(2)}) collective-permute-start(f32[88,128]{1,0:T(8,128)S(1)} %fusion.1.mine), channel_id=1, source_target_pairs={{0,4},{4,0},{1,5},{5,1},{2,6},{6,2},{3,7},{7,3},{8,12},{12,8},{9,1... | collective-permute-start | bytes 135176 | tf_op jit(solution)/shard_map/ppermute | solution.py:383
  50.0 8.5 %collective-permute-start.10 = (bf16[32,16,128]{2,1,0:T(8,128)(2,1)S(1)}, bf16[32,16,128]{2,1,0:T(8,128)(2,1)S(1)}, u32[]{:S(2)}, u32[]{:S(2)}) collective-permute-start(bf16[32,16,128]{2,1,0:T(8,128)(2,1)S(1)} %get-tuple-element.39), channel_id=1, source_target_pairs={{0,8},{8,0},{16,24},{24,16},{1,9},{9,1},{17,25},{25,17},{2,10},{10... | collective-permute-start | bytes 393224 | tf_op jit(solution)/shard_map/ppermute | solution.py:383
  51.0 7.5 %collective-permute-start.11 = (bf16[32,16,128]{2,1,0:T(8,128)(2,1)S(1)}, bf16[32,16,128]{2,1,0:T(8,128)(2,1)S(1)}, u32[]{:S(2)}, u32[]{:S(2)}) collective-permute-start(bf16[32,16,128]{2,1,0:T(8,128)(2,1)S(1)} %get-tuple-element.40), channel_id=1, source_target_pairs={{0,1},{1,0},{2,3},{3,2},{8,16},{9,17},{10,18},{11,19},{16,8},{17,9... | collective-permute-start | bytes 393224 | tf_op jit(solution)/shard_map/ppermute | solution.py:405
  52.3 6.1 %collective-permute-start.12 = (f32[128,128]{1,0:T(8,128)S(1)}, f32[128,128]{1,0:T(8,128)S(1)}, u32[]{:S(2)}, u32[]{:S(2)}) collective-permute-start(f32[128,128]{1,0:T(8,128)S(1)} %get-tuple-element.41), channel_id=1, source_target_pairs={{0,4},{4,0},{1,5},{5,1},{2,6},{6,2},{3,7},{7,3},{8,12},{12,8},{9,1... | collective-permute-start | bytes 196616 | tf_op jit(solution)/shard_map/ppermute | solution.py:383
  52.3 6.1 %collective-permute-start.14 = (f32[64,128]{1,0:T(8,128)S(1)}, f32[64,128]{1,0:T(8,128)S(1)}, u32[]{:S(2)}, u32[]{:S(2)}) collective-permute-start(f32[64,128]{1,0:T(8,128)S(1)} %get-tuple-element.42), channel_id=1, source_target_pairs={{0,8},{8,0},{16,24},{24,16},{1,2},{9,10},{17,18},{25,26},{2,1},{10... | collective-permute-start | bytes 98312 | tf_op jit(solution)/shard_map/ppermute | solution.py:405
  53.1 5.4 %collective-permute-start.13 = (f32[64,128]{1,0:T(8,128)S(1)}, f32[64,128]{1,0:T(8,128)S(1)}, u32[]{:S(2)}, u32[]{:S(2)}) collective-permute-start(f32[64,128]{1,0:T(8,128)S(1)} %get-tuple-element.42), channel_id=1, source_target_pairs={{0,1},{1,0},{2,3},{3,2},{4,5},{5,4},{6,7},{7,6},{8,9},{9,8},{10,11... | collective-permute-start | bytes 98312 | tf_op jit(solution)/shard_map/ppermute | solution.py:383
  71.2 1.3 %collective-permute-start.15 = (f32[216,128]{1,0:T(8,128)S(1)}, f32[216,128]{1,0:T(8,128)S(1)}, u32[]{:S(2)}, u32[]{:S(2)}) collective-permute-start(f32[216,128]{1,0:T(8,128)S(1)} %get-tuple-element.44), channel_id=1, source_target_pairs={{0,4},{4,0},{1,5},{5,1},{2,6},{6,2},{3,7},{7,3},{8,12},{12,8},{9,1... | collective-permute-start | bytes 331784 | tf_op jit(solution)/shard_map/ppermute | solution.py:383
  72.6 4.1 %collective-permute-start.18 = (f32[88,128]{1,0:T(8,128)S(1)}, f32[88,128]{1,0:T(8,128)S(1)}, u32[]{:S(2)}, u32[]{:S(2)}) collective-permute-start(f32[88,128]{1,0:T(8,128)S(1)} %slice_add_fusion.2), channel_id=1, source_target_pairs={{0,16},{8,24},{16,0},{24,8},{1,17},{9,25},{17,1},{25,9},{2,18},{10... | collective-permute-start | bytes 135176 | tf_op jit(solution)/shard_map/ppermute | solution.py:383
  73.7 4.9 %collective-permute-start.17 = (f32[88,128]{1,0:T(8,128)S(1)}, f32[88,128]{1,0:T(8,128)S(1)}, u32[]{:S(2)}, u32[]{:S(2)}) collective-permute-start(f32[88,128]{1,0:T(8,128)S(1)} %slice_add_fusion.2), channel_id=1, source_target_pairs={{0,24},{8,16},{16,8},{24,0},{1,25},{9,17},{17,9},{25,1},{2,26},{10... | collective-permute-start | bytes 135176 | tf_op jit(solution)/shard_map/ppermute | solution.py:383
  75.1 4.0 %collective-permute-start.16 = (f32[88,128]{1,0:T(8,128)S(1)}, f32[88,128]{1,0:T(8,128)S(1)}, u32[]{:S(2)}, u32[]{:S(2)}) collective-permute-start(f32[88,128]{1,0:T(8,128)S(1)} %slice_add_fusion.2), channel_id=1, source_target_pairs={{0,8},{8,0},{16,24},{24,16},{1,9},{9,1},{17,25},{25,17},{2,10},{10... | collective-permute-start | bytes 135176 | tf_op jit(solution)/shard_map/ppermute | solution.py:383
  79.2 7.7 %collective-permute-start.20 = (f32[152,128]{1,0:T(8,128)S(1)}, f32[152,128]{1,0:T(8,128)S(1)}, u32[]{:S(2)}, u32[]{:S(2)}) collective-permute-start(f32[152,128]{1,0:T(8,128)S(1)} %constant_dynamic-update-slice_fusion.2), channel_id=1, source_target_pairs={{0,3},{1,2},{2,1},{3,0},{4,7},{5,6},{6,5},{7,4},{8,11},{9,10},{10,... | collective-permute-start | bytes 233480 | tf_op jit(solution)/shard_map/ppermute | solution.py:383
  81.1 6.6 %collective-permute-start.19 = (f32[152,128]{1,0:T(8,128)S(1)}, f32[152,128]{1,0:T(8,128)S(1)}, u32[]{:S(2)}, u32[]{:S(2)}) collective-permute-start(f32[152,128]{1,0:T(8,128)S(1)} %constant_dynamic-update-slice_fusion.2), channel_id=1, source_target_pairs={{0,1},{1,0},{2,3},{3,2},{4,5},{5,4},{6,7},{7,6},{8,9},{9,8},{10,11... | collective-permute-start | bytes 233480 | tf_op jit(solution)/shard_map/ppermute | solution.py:383
  81.8 5.1 %collective-permute-start.21 = (f32[88,128]{1,0:T(8,128)S(1)}, f32[88,128]{1,0:T(8,128)S(1)}, u32[]{:S(2)}, u32[]{:S(2)}) collective-permute-start(f32[88,128]{1,0:T(8,128)S(1)} %add_add_fusion), channel_id=1, source_target_pairs={{0,2},{1,3},{2,0},{3,1},{4,6},{5,7},{6,4},{7,5},{8,10},{9,11},{10,... | collective-permute-start | bytes 135176 | tf_op jit(solution)/shard_map/ppermute | solution.py:383
  83.6 5.4 %collective-permute-start.23 = (bf16[32,16,128]{2,1,0:T(8,128)(2,1)S(1)}, bf16[32,16,128]{2,1,0:T(8,128)(2,1)S(1)}, u32[]{:S(2)}, u32[]{:S(2)}) collective-permute-start(bf16[32,16,128]{2,1,0:T(8,128)(2,1)S(1)} %get-tuple-element.50), channel_id=1, source_target_pairs={{0,8},{8,0},{16,24},{24,16},{1,9},{9,1},{17,25},{25,17},{2,10},{10... | collective-permute-start | bytes 393224 | tf_op jit(solution)/shard_map/ppermute | solution.py:383
  84.7 5.0 %collective-permute-start.24 = (bf16[32,16,128]{2,1,0:T(8,128)(2,1)S(1)}, bf16[32,16,128]{2,1,0:T(8,128)(2,1)S(1)}, u32[]{:S(2)}, u32[]{:S(2)}) collective-permute-start(bf16[32,16,128]{2,1,0:T(8,128)(2,1)S(1)} %get-tuple-element.51), channel_id=1, source_target_pairs={{0,1},{1,0},{2,3},{3,2},{8,16},{9,17},{10,18},{11,19},{16,8},{17,9... | collective-permute-start | bytes 393224 | tf_op jit(solution)/shard_map/ppermute | solution.py:405
  87.7 1.3 %collective-permute-start.22 = (f32[88,128]{1,0:T(8,128)S(1)}, f32[88,128]{1,0:T(8,128)S(1)}, u32[]{:S(2)}, u32[]{:S(2)}) collective-permute-start(f32[88,128]{1,0:T(8,128)S(1)} %fusion.mine), channel_id=1, source_target_pairs={{0,4},{4,0},{1,5},{5,1},{2,6},{6,2},{3,7},{7,3},{8,12},{12,8},{9,1... | collective-permute-start | bytes 135176 | tf_op jit(solution)/shard_map/ppermute | solution.py:383
where the time goes:
time: 103 us; the launch traced here: 102 us
  Pallas kernels  52.2 us (51%)
  starting transfers between devices  26.8 us (26%)
  waiting for transfers between devices  21.2 us (21%)
  local copies, waits for them, and re-layouts  1.33 us (1%)
    pallas_call x4, Pallas kernels, call(): pl.pallas_call(kernel, out_shape=tuple(outs), in_specs=specs, out_specs=t...  52.2 us
    ppermute x21, starting transfers between devices, send(): return lax.ppermute(value, axis, list(enumerate(to)))  23.2 us
    ppermute x21, waiting for transfers between devices, send(): return lax.ppermute(value, axis, list(enumerate(to)))  17.2 us
    ppermute x4, waiting for transfers between devices, send_middle(): return lax.ppermute(value, ('gx', 'gz'), pairs)  4.03 us
    ppermute x4, starting transfers between devices, send_middle(): return lax.ppermute(value, ('gx', 'gz'), pairs)  3.59 us
  transfers between devices with their start and end apart: 25, of which 17 were waited for; matrix products, arithmetic and copies ran while one was open for 0% of the time, Pallas kernels for 0%

commit v1 on v0

--- a/solution.py
+++ b/solution.py
@@ -13,7 +13,6 @@
 PIVOTS = 8
 VOXEL_ROWS = 8
 CHUNK = 8
-SPLIT = 2
 TOGETHER = {"first": 4, "near": 8, "second": 4, "third": 8, "fourth": 4}
 f32, bf16 = jnp.float32, jnp.bfloat16
 
@@ -28,33 +27,36 @@
 
 def moments_of(x, q):
     ny, feats, _ = x.shape
-    scatter = first = None
-    chunk, part = CHUNK, feats // SPLIT
-    for c in range(0, ny, chunk):
-        xs = jnp.concatenate([x[y] for y in range(c, c + chunk)], axis=1)
-        qs = jnp.concatenate([q[y] for y in range(c, c + chunk)], axis=1)
+    last = feats - 128 // q.shape[1]
+    sums = None
+    for c in range(0, ny, CHUNK):
+        xs = jnp.concatenate([x[y] for y in range(c, c + CHUNK)], axis=1)
+        qs = jnp.concatenate([q[y] for y in range(c, c + CHUNK)], axis=1)
         ones = jnp.ones((16, xs.shape[1]), bf16)
-        s = []
-        for g in range(0, feats, part):
-            weighted = jnp.concatenate([xs[f : f + 1] * qs for f in range(g, g + part)], axis=0)
-            s.append(lax.dot_general(xs, weighted, ROWS_ROWS, preferred_element_type=f32))
-        s = jnp.concatenate(s, axis=1)
-        m = lax.dot_general(
-            jnp.concatenate([xs, ones], axis=0), qs, ROWS_ROWS, preferred_element_type=f32
+        weighted = [xs[f : f + 1] * qs for f in range(feats)]
+        here = (
+            lax.dot_general(xs, jnp.concatenate(weighted[:last], axis=0), ROWS_ROWS, preferred_element_type=f32),
+            lax.dot_general(
+                jnp.concatenate([*weighted[last:], qs], axis=0),
+                jnp.concatenate([xs, ones], axis=0),
+                ROWS_ROWS,
+                preferred_element_type=f32,
+            ),
         )
-        scatter = s if scatter is None else scatter + s
-        first = m if first is None else first + m
-    return scatter, first
+        sums = here if sums is None else jax.tree.map(jnp.add, sums, here)
+    return sums
 
 
 def no_moments(feats, classes):
-    return jnp.zeros((feats, feats * classes), f32), jnp.zeros((feats + 16, classes), f32)
-
-
-def put_moments(place_ref, mine, theirs, scatter, first):
+    return jnp.zeros((feats, feats * classes - 128), f32), jnp.zeros((128 + classes, feats + 16), f32)
+
+
+def put_moments(place_ref, mine, theirs, scatter, rest):
     feats, lanes = scatter.shape
     rows = [scatter[:, j : j + 128] for j in range(0, lanes, 128)]
-    rows.append(jnp.pad(first[: feats + 8], ((0, 0), (0, 128 - first.shape[1]))))
+    rest = jnp.pad(rest, ((0, 256 - rest.shape[0]), (0, 128 - rest.shape[1])))
+    rows.append(rest[:128].T[:feats])
+    rows.append(rest[128:].T[: feats + 8])
     half = mine.shape[0]
     rows.append(jnp.zeros((2 * half - sum(r.shape[0] for r in rows), 128), f32))
     rows = jnp.concatenate(rows, axis=0)

time: 103 us -> 100 us (0.971)
  Pallas kernels: 52.2 us -> 49.8 us
    pallas_call x4, Pallas kernels: 52.2 us -> 49.8 us  [call(): pl.pallas_call(kernel, out_shape=tuple(outs), in_specs=specs, out_specs=t...]
where the time goes in v1:
time: 100 us
  Pallas kernels  49.8 us (50%)
  starting transfers between devices  26.8 us (27%)
  waiting for transfers between devices  21.3 us (21%)
  local copies, waits for them, and re-layouts  1.33 us (1%)
    pallas_call x4, Pallas kernels, call(): pl.pallas_call(kernel, out_shape=tuple(outs), in_specs=specs, out_specs=t...  49.8 us
    ppermute x21, starting transfers between devices, send(): return lax.ppermute(value, axis, list(enumerate(to)))  23.3 us
    ppermute x21, waiting for transfers between devices, send(): return lax.ppermute(value, axis, list(enumerate(to)))  17.2 us
    ppermute x4, waiting for transfers between devices, send_middle(): return lax.ppermute(value, ('gx', 'gz'), pairs)  4.03 us
    ppermute x4, starting transfers between devices, send_middle(): return lax.ppermute(value, ('gx', 'gz'), pairs)  3.57 us
  transfers between devices with their start and end apart: 25, of which 17 were waited for; matrix products, arithmetic and copies ran while one was open for 0% of the time, Pallas kernels for 0%

profile of v1, /device:TPU:0, one launch (start us, length us, event | category | flops | bytes accessed | tf_op | source)
XLA Modules:
  0.0 100.1 jit_solution(6337100143283465464)
XLA Ops:
  0.7 0.1 stack.66.place
  0.8 0.0 copy-start
  0.8 1.2 %copy-done = bf16[16,8,32,128]{3,2,1,0:T(8,128)(2,1)S(1)} copy-done((bf16[16,8,32,128]{3,2,1,0:T(8,128)(2,1)S(1)}, bf16[16,8,32,128]{3,2,1,0:T(8,128)(2,1)}, u32[]{:S(2)}) %copy-start) | copy-done | bytes 1048600
  2.0 12.1 %shard_map.41 = (bf16[8,32,32,128]{3,2,1,0:T(8,128)(2,1)S(1)}, bf16[8,32,16,128]{3,2,1,0:T(8,128)(2,1)S(1)}, bf16[32,16,128]{2,1,0:T(8,128)(2,1)S(1)}, bf16[32,1...) custom-call(s32[12]{0:T(128)S(1)} %stack.66.place, ...), custom_call_target="tpu_custom_call" | custom-call | tf_op jit(solution)/shard_map/pallas_call | solution.py:454
  14.1 0.5 collective-permute-start
  14.6 1.0 collective-permute-done.yi.yo
  15.6 2.9 %collective-permute-start.3 = (f32[88,128]{1,0:T(8,128)S(1)}, f32[88,128]{1,0:T(8,128)S(1)}, u32[]{:S(2)}, u32[]{:S(2)}) collective-permute-start(f32[88,128]{1,0:T(8,128)S(1)} %slice_add_fusion.5), channel_id=1, source_target_pairs={{0,16},{8,24},{16,0},{24,8},{1,17},{9,25},{17,1},{25,9},{2,18},{10... | collective-permute-start | bytes 135176 | tf_op jit(solution)/shard_map/ppermute | solution.py:385
  18.5 1.4 %collective-permute-start.2 = (f32[88,128]{1,0:T(8,128)S(1)}, f32[88,128]{1,0:T(8,128)S(1)}, u32[]{:S(2)}, u32[]{:S(2)}) collective-permute-start(f32[88,128]{1,0:T(8,128)S(1)} %slice_add_fusion.5), channel_id=1, source_target_pairs={{0,24},{8,16},{16,8},{24,0},{1,25},{9,17},{17,9},{25,1},{2,26},{10... | collective-permute-start | bytes 135176 | tf_op jit(solution)/shard_map/ppermute | solution.py:385
  19.9 0.1 collective-permute-start.1
  20.0 0.5 collective-permute-done.3
  20.6 3.3 %collective-permute-done.2 = f32[88,128]{1,0:T(8,128)S(1)} collective-permute-done((f32[88,128]{1,0:T(8,128)S(1)}, f32[88,128]{1,0:T(8,128)S(1)}, u32[]{:S(2)}, u32[]{:S(2)}) %collective-permute-start.2) | collective-permute-done | bytes 45088 | tf_op jit(solution)/shard_map/ppermute | solution.py:385
  23.9 0.1 collective-permute-done.1
  24.0 3.7 %collective-permute-start.5 = (f32[152,128]{1,0:T(8,128)S(1)}, f32[152,128]{1,0:T(8,128)S(1)}, u32[]{:S(2)}, u32[]{:S(2)}) collective-permute-start(f32[152,128]{1,0:T(8,128)S(1)} %constant_dynamic-update-slice_fusion), channel_id=1, source_target_pairs={{0,3},{1,2},{2,1},{3,0},{4,7},{5,6},{6,5},{7,4},{8,11},{9,10},{10,... | collective-permute-start | bytes 233480 | tf_op jit(solution)/shard_map/ppermute | solution.py:385
  27.7 0.0 collective-permute-start.4
  27.7 0.8 collective-permute-start.6
  28.5 1.0 collective-permute-start.8
  29.4 1.2 %collective-permute-start.9 = (bf16[32,16,128]{2,1,0:T(8,128)(2,1)S(1)}, bf16[32,16,128]{2,1,0:T(8,128)(2,1)S(1)}, u32[]{:S(2)}, u32[]{:S(2)}) collective-permute-start(bf16[32,16,128]{2,1,0:T(8,128)(2,1)S(1)} %get-tuple-element.36), channel_id=1, source_target_pairs={{0,1},{1,0},{2,3},{3,2},{8,16},{9,17},{10,18},{11,19},{16,8},{17,9... | collective-permute-start | bytes 393224 | tf_op jit(solution)/shard_map/ppermute | solution.py:407
  30.7 2.1 %collective-permute-done.6 = f32[88,128]{1,0:T(8,128)S(1)} collective-permute-done((f32[88,128]{1,0:T(8,128)S(1)}, f32[88,128]{1,0:T(8,128)S(1)}, u32[]{:S(2)}, u32[]{:S(2)}) %collective-permute-start.6) | collective-permute-done | bytes 45088 | tf_op jit(solution)/shard_map/ppermute | solution.py:385
  32.7 0.0 collective-permute-done.5.zo
  32.7 0.7 collective-permute-done.4.zi
  33.5 0.1 collective-permute-start.7
  33.6 1.2 %collective-permute-done.7.theirs = f32[88,128]{1,0:T(8,128)S(1)} collective-permute-done((f32[88,128]{1,0:T(8,128)S(1)}, f32[88,128]{1,0:T(8,128)S(1)}, u32[]{:S(2)}, u32[]{:S(2)}) %collective-permute-start.7) | collective-permute-done | bytes 45088 | tf_op jit(solution)/shard_map/ppermute | solution.py:385
  34.8 0.0 collective-permute-done.8.xi
  34.8 0.6 collective-permute-done.9.xo
  35.4 12.8 %shard_map.42 = (f32[8,32,16,128]{3,2,1,0:T(8,128)S(1)}, bf16[8,32,16,128]{3,2,1,0:T(8,128)(2,1)S(1)}, bf16[32,16,128]{2,1,0:T(8,128)(2,1)S(1)}, bf16[32,16,128]...) custom-call(s32[12]{0:T(128)S(1)} %stack.66.place, ...), custom_call_target="tpu_custom_call" | custom-call | tf_op jit(solution)/shard_map/pallas_call | solution.py:454
  48.1 1.0 collective-permute-start.10
  49.1 1.3 %collective-permute-start.11 = (bf16[32,16,128]{2,1,0:T(8,128)(2,1)S(1)}, bf16[32,16,128]{2,1,0:T(8,128)(2,1)S(1)}, u32[]{:S(2)}, u32[]{:S(2)}) collective-permute-start(bf16[32,16,128]{2,1,0:T(8,128)(2,1)S(1)} %get-tuple-element.40), channel_id=1, source_target_pairs={{0,1},{1,0},{2,3},{3,2},{8,16},{9,17},{10,18},{11,19},{16,8},{17,9... | collective-permute-start | bytes 393224 | tf_op jit(solution)/shard_map/ppermute | solution.py:407
  50.5 0.0 collective-permute-start.12
  50.5 0.7 collective-permute-start.14
  51.2 2.6 %collective-permute-start.13 = (f32[64,128]{1,0:T(8,128)S(1)}, f32[64,128]{1,0:T(8,128)S(1)}, u32[]{:S(2)}, u32[]{:S(2)}) collective-permute-start(f32[64,128]{1,0:T(8,128)S(1)} %get-tuple-element.42), channel_id=1, source_target_pairs={{0,1},{1,0},{2,3},{3,2},{4,5},{5,4},{6,7},{7,6},{8,9},{9,8},{10,11... | collective-permute-start | bytes 98312 | tf_op jit(solution)/shard_map/ppermute | solution.py:385
  53.8 2.8 %collective-permute-done.14.zo = f32[64,128]{1,0:T(8,128)S(1)} collective-permute-done((f32[64,128]{1,0:T(8,128)S(1)}, f32[64,128]{1,0:T(8,128)S(1)}, u32[]{:S(2)}, u32[]{:S(2)}) %collective-permute-start.14) | collective-permute-done | bytes 32800 | tf_op jit(solution)/shard_map/ppermute | solution.py:407
  56.6 0.0 collective-permute-done.13.zi
  56.6 0.0 collective-permute-done.12.yi.yo
  56.6 0.0 collective-permute-done.10.xi
  56.6 0.0 collective-permute-done.11.xo
  56.6 12.2 %shard_map.43 = (bf16[8,32,16,128]{3,2,1,0:T(8,128)(2,1)S(1)}, bf16[32,16,128]{2,1,0:T(8,128)(2,1)S(1)}, bf16[32,16,128]{2,1,0:T(8,128)(2,1)S(1)}, f32[128,128]{...) custom-call(s32[12]{0:T(128)S(1)} %stack.66.place, ...), custom_call_target="tpu_custom_call" | custom-call | tf_op jit(solution)/shard_map/pallas_call | solution.py:454
  68.8 0.1 collective-permute-start.15
  68.9 1.3 %collective-permute-done.15.yi.yo = f32[216,128]{1,0:T(8,128)S(1)} collective-permute-done((f32[216,128]{1,0:T(8,128)S(1)}, f32[216,128]{1,0:T(8,128)S(1)}, u32[]{:S(2)}, u32[]{:S(2)}) %collective-permute-start.15) | collective-permute-done | bytes 110624 | tf_op jit(solution)/shard_map/ppermute | solution.py:385
  70.2 1.1 %collective-permute-start.18 = (f32[88,128]{1,0:T(8,128)S(1)}, f32[88,128]{1,0:T(8,128)S(1)}, u32[]{:S(2)}, u32[]{:S(2)}) collective-permute-start(f32[88,128]{1,0:T(8,128)S(1)} %slice_add_fusion.2), channel_id=1, source_target_pairs={{0,16},{8,24},{16,0},{24,8},{1,17},{9,25},{17,1},{25,9},{2,18},{10... | collective-permute-start | bytes 135176 | tf_op jit(solution)/shard_map/ppermute | solution.py:385
  71.3 1.4 %collective-permute-start.17 = (f32[88,128]{1,0:T(8,128)S(1)}, f32[88,128]{1,0:T(8,128)S(1)}, u32[]{:S(2)}, u32[]{:S(2)}) collective-permute-start(f32[88,128]{1,0:T(8,128)S(1)} %slice_add_fusion.2), channel_id=1, source_target_pairs={{0,24},{8,16},{16,8},{24,0},{1,25},{9,17},{17,9},{25,1},{2,26},{10... | collective-permute-start | bytes 135176 | tf_op jit(solution)/shard_map/ppermute | solution.py:385
  72.7 1.0 %collective-permute-start.16 = (f32[88,128]{1,0:T(8,128)S(1)}, f32[88,128]{1,0:T(8,128)S(1)}, u32[]{:S(2)}, u32[]{:S(2)}) collective-permute-start(f32[88,128]{1,0:T(8,128)S(1)} %slice_add_fusion.2), channel_id=1, source_target_pairs={{0,8},{8,0},{16,24},{24,16},{1,9},{9,1},{17,25},{25,17},{2,10},{10... | collective-permute-start | bytes 135176 | tf_op jit(solution)/shard_map/ppermute | solution.py:385
  73.7 0.6 collective-permute-done.18
  74.3 2.0 %collective-permute-done.17 = f32[88,128]{1,0:T(8,128)S(1)} collective-permute-done((f32[88,128]{1,0:T(8,128)S(1)}, f32[88,128]{1,0:T(8,128)S(1)}, u32[]{:S(2)}, u32[]{:S(2)}) %collective-permute-start.17) | collective-permute-done | bytes 45088 | tf_op jit(solution)/shard_map/ppermute | solution.py:385
  76.3 0.5 collective-permute-done.16
  76.8 1.9 %collective-permute-start.20 = (f32[152,128]{1,0:T(8,128)S(1)}, f32[152,128]{1,0:T(8,128)S(1)}, u32[]{:S(2)}, u32[]{:S(2)}) collective-permute-start(f32[152,128]{1,0:T(8,128)S(1)} %constant_dynamic-update-slice_fusion.2), channel_id=1, source_target_pairs={{0,3},{1,2},{2,1},{3,0},{4,7},{5,6},{6,5},{7,4},{8,11},{9,10},{10,... | collective-permute-start | bytes 233480 | tf_op jit(solution)/shard_map/ppermute | solution.py:385
  78.7 0.7 collective-permute-start.19
  79.4 1.8 %collective-permute-start.21 = (f32[88,128]{1,0:T(8,128)S(1)}, f32[88,128]{1,0:T(8,128)S(1)}, u32[]{:S(2)}, u32[]{:S(2)}) collective-permute-start(f32[88,128]{1,0:T(8,128)S(1)} %add_add_fusion), channel_id=1, source_target_pairs={{0,2},{1,3},{2,0},{3,1},{4,6},{5,7},{6,4},{7,5},{8,10},{9,11},{10,... | collective-permute-start | bytes 135176 | tf_op jit(solution)/shard_map/ppermute | solution.py:385
  81.2 1.0 %collective-permute-start.23 = (bf16[32,16,128]{2,1,0:T(8,128)(2,1)S(1)}, bf16[32,16,128]{2,1,0:T(8,128)(2,1)S(1)}, u32[]{:S(2)}, u32[]{:S(2)}) collective-permute-start(bf16[32,16,128]{2,1,0:T(8,128)(2,1)S(1)} %get-tuple-element.50), channel_id=1, source_target_pairs={{0,8},{8,0},{16,24},{24,16},{1,9},{9,1},{17,25},{25,17},{2,10},{10... | collective-permute-start | bytes 393224 | tf_op jit(solution)/shard_map/ppermute | solution.py:385
  82.3 0.2 collective-permute-start.24
  82.5 2.0 %collective-permute-done.21 = f32[88,128]{1,0:T(8,128)S(1)} collective-permute-done((f32[88,128]{1,0:T(8,128)S(1)}, f32[88,128]{1,0:T(8,128)S(1)}, u32[]{:S(2)}, u32[]{:S(2)}) %collective-permute-start.21) | collective-permute-done | bytes 45088 | tf_op jit(solution)/shard_map/ppermute | solution.py:385
  84.5 0.0 collective-permute-done.20.zo
  84.5 0.8 collective-permute-done.19.zi
  85.3 0.1 collective-permute-start.22
  85.4 1.2 %collective-permute-done.22.theirs = f32[88,128]{1,0:T(8,128)S(1)} collective-permute-done((f32[88,128]{1,0:T(8,128)S(1)}, f32[88,128]{1,0:T(8,128)S(1)}, u32[]{:S(2)}, u32[]{:S(2)}) %collective-permute-start.22) | collective-permute-done | bytes 45088 | tf_op jit(solution)/shard_map/ppermute | solution.py:385
  86.6 0.0 collective-permute-done.23.xi
  86.6 0.7 collective-permute-done.24.xo
  87.3 12.8 %shard_map.44 = (bf16[16,8,32,128]{3,2,1,0:T(8,128)(2,1)}, f32[16,32]{1,0:T(8,128)}) custom-call(s32[12]{0:T(128)S(1)} %stack.66.place, f32[88,128]{1,0:T(8,128)S(1)} %fusion.mine, f32[88,128]{1,0:T(8,128)S(1)} %collective-permute-done.22.theirs, bf16[8,32,32,128]{3,2,1,0:T(8,128)(2,1)S(1)} %get-tuple-element.33.xt, ...), custom_call_target="tpu_custom_call" | custom-call | tf_op jit(solution)/shard_map/pallas_call | solution.py:454
  (10 shorter events, 0.1 us)
Async XLA Ops:
  0.8 1.2 %copy-start = (bf16[16,8,32,128]{3,2,1,0:T(8,128)(2,1)S(1)}, bf16[16,8,32,128]{3,2,1,0:T(8,128)(2,1)}, u32[]{:S(2)}) copy-start(bf16[16,8,32,128]{3,2,1,0:T(8,128)(2,1)} %q_hbm.1) | copy-start | bytes 3145732
  14.1 1.5 %collective-permute-start = (f32[216,128]{1,0:T(8,128)S(1)}, f32[216,128]{1,0:T(8,128)S(1)}, u32[]{:S(2)}, u32[]{:S(2)}) collective-permute-start(f32[216,128]{1,0:T(8,128)S(1)} %get-tuple-element.28), channel_id=1, source_target_pairs={{0,4},{4,0},{1,5},{5,1},{2,6},{6,2},{3,7},{7,3},{8,12},{12,8},{9,1... | collective-permute-start | bytes 331784 | tf_op jit(solution)/shard_map/ppermute | solution.py:385
  15.6 5.0 %collective-permute-start.3 = (f32[88,128]{1,0:T(8,128)S(1)}, f32[88,128]{1,0:T(8,128)S(1)}, u32[]{:S(2)}, u32[]{:S(2)}) collective-permute-start(f32[88,128]{1,0:T(8,128)S(1)} %slice_add_fusion.5), channel_id=1, source_target_pairs={{0,16},{8,24},{16,0},{24,8},{1,17},{9,25},{17,1},{25,9},{2,18},{10... | collective-permute-start | bytes 135176 | tf_op jit(solution)/shard_map/ppermute | solution.py:385
  18.5 5.4 %collective-permute-start.2 = (f32[88,128]{1,0:T(8,128)S(1)}, f32[88,128]{1,0:T(8,128)S(1)}, u32[]{:S(2)}, u32[]{:S(2)}) collective-permute-start(f32[88,128]{1,0:T(8,128)S(1)} %slice_add_fusion.5), channel_id=1, source_target_pairs={{0,24},{8,16},{16,8},{24,0},{1,25},{9,17},{17,9},{25,1},{2,26},{10... | collective-permute-start | bytes 135176 | tf_op jit(solution)/shard_map/ppermute | solution.py:385
  19.9 4.0 %collective-permute-start.1 = (f32[88,128]{1,0:T(8,128)S(1)}, f32[88,128]{1,0:T(8,128)S(1)}, u32[]{:S(2)}, u32[]{:S(2)}) collective-permute-start(f32[88,128]{1,0:T(8,128)S(1)} %slice_add_fusion.5), channel_id=1, source_target_pairs={{0,8},{8,0},{16,24},{24,16},{1,9},{9,1},{17,25},{25,17},{2,10},{10... | collective-permute-start | bytes 135176 | tf_op jit(solution)/shard_map/ppermute | solution.py:385
  24.0 8.7 %collective-permute-start.5 = (f32[152,128]{1,0:T(8,128)S(1)}, f32[152,128]{1,0:T(8,128)S(1)}, u32[]{:S(2)}, u32[]{:S(2)}) collective-permute-start(f32[152,128]{1,0:T(8,128)S(1)} %constant_dynamic-update-slice_fusion), channel_id=1, source_target_pairs={{0,3},{1,2},{2,1},{3,0},{4,7},{5,6},{6,5},{7,4},{8,11},{9,10},{10,... | collective-permute-start | bytes 233480 | tf_op jit(solution)/shard_map/ppermute | solution.py:385
  27.7 5.8 %collective-permute-start.4 = (f32[152,128]{1,0:T(8,128)S(1)}, f32[152,128]{1,0:T(8,128)S(1)}, u32[]{:S(2)}, u32[]{:S(2)}) collective-permute-start(f32[152,128]{1,0:T(8,128)S(1)} %constant_dynamic-update-slice_fusion), channel_id=1, source_target_pairs={{0,1},{1,0},{2,3},{3,2},{4,5},{5,4},{6,7},{7,6},{8,9},{9,8},{10,11... | collective-permute-start | bytes 233480 | tf_op jit(solution)/shard_map/ppermute | solution.py:385
  27.7 5.1 %collective-permute-start.6 = (f32[88,128]{1,0:T(8,128)S(1)}, f32[88,128]{1,0:T(8,128)S(1)}, u32[]{:S(2)}, u32[]{:S(2)}) collective-permute-start(f32[88,128]{1,0:T(8,128)S(1)} %add_add_fusion.1), channel_id=1, source_target_pairs={{0,2},{1,3},{2,0},{3,1},{4,6},{5,7},{6,4},{7,5},{8,10},{9,11},{10,... | collective-permute-start | bytes 135176 | tf_op jit(solution)/shard_map/ppermute | solution.py:385
  28.5 6.3 %collective-permute-start.8 = (bf16[32,16,128]{2,1,0:T(8,128)(2,1)S(1)}, bf16[32,16,128]{2,1,0:T(8,128)(2,1)S(1)}, u32[]{:S(2)}, u32[]{:S(2)}) collective-permute-start(bf16[32,16,128]{2,1,0:T(8,128)(2,1)S(1)} %get-tuple-element.35), channel_id=1, source_target_pairs={{0,8},{8,0},{16,24},{24,16},{1,9},{9,1},{17,25},{25,17},{2,10},{10... | collective-permute-start | bytes 393224 | tf_op jit(solution)/shard_map/ppermute | solution.py:385
  29.4 5.9 %collective-permute-start.9 = (bf16[32,16,128]{2,1,0:T(8,128)(2,1)S(1)}, bf16[32,16,128]{2,1,0:T(8,128)(2,1)S(1)}, u32[]{:S(2)}, u32[]{:S(2)}) collective-permute-start(bf16[32,16,128]{2,1,0:T(8,128)(2,1)S(1)} %get-tuple-element.36), channel_id=1, source_target_pairs={{0,1},{1,0},{2,3},{3,2},{8,16},{9,17},{10,18},{11,19},{16,8},{17,9... | collective-permute-start | bytes 393224 | tf_op jit(solution)/shard_map/ppermute | solution.py:407
  33.5 1.3 %collective-permute-start.7 = (f32[88,128]{1,0:T(8,128)S(1)}, f32[88,128]{1,0:T(8,128)S(1)}, u32[]{:S(2)}, u32[]{:S(2)}) collective-permute-start(f32[88,128]{1,0:T(8,128)S(1)} %fusion.1.mine), channel_id=1, source_target_pairs={{0,4},{4,0},{1,5},{5,1},{2,6},{6,2},{3,7},{7,3},{8,12},{12,8},{9,1... | collective-permute-start | bytes 135176 | tf_op jit(solution)/shard_map/ppermute | solution.py:385
  48.1 8.5 %collective-permute-start.10 = (bf16[32,16,128]{2,1,0:T(8,128)(2,1)S(1)}, bf16[32,16,128]{2,1,0:T(8,128)(2,1)S(1)}, u32[]{:S(2)}, u32[]{:S(2)}) collective-permute-start(bf16[32,16,128]{2,1,0:T(8,128)(2,1)S(1)} %get-tuple-element.39), channel_id=1, source_target_pairs={{0,8},{8,0},{16,24},{24,16},{1,9},{9,1},{17,25},{25,17},{2,10},{10... | collective-permute-start | bytes 393224 | tf_op jit(solution)/shard_map/ppermute | solution.py:385
  49.1 7.5 %collective-permute-start.11 = (bf16[32,16,128]{2,1,0:T(8,128)(2,1)S(1)}, bf16[32,16,128]{2,1,0:T(8,128)(2,1)S(1)}, u32[]{:S(2)}, u32[]{:S(2)}) collective-permute-start(bf16[32,16,128]{2,1,0:T(8,128)(2,1)S(1)} %get-tuple-element.40), channel_id=1, source_target_pairs={{0,1},{1,0},{2,3},{3,2},{8,16},{9,17},{10,18},{11,19},{16,8},{17,9... | collective-permute-start | bytes 393224 | tf_op jit(solution)/shard_map/ppermute | solution.py:407
  50.5 6.1 %collective-permute-start.12 = (f32[128,128]{1,0:T(8,128)S(1)}, f32[128,128]{1,0:T(8,128)S(1)}, u32[]{:S(2)}, u32[]{:S(2)}) collective-permute-start(f32[128,128]{1,0:T(8,128)S(1)} %get-tuple-element.41), channel_id=1, source_target_pairs={{0,4},{4,0},{1,5},{5,1},{2,6},{6,2},{3,7},{7,3},{8,12},{12,8},{9,1... | collective-permute-start | bytes 196616 | tf_op jit(solution)/shard_map/ppermute | solution.py:385
  50.5 6.1 %collective-permute-start.14 = (f32[64,128]{1,0:T(8,128)S(1)}, f32[64,128]{1,0:T(8,128)S(1)}, u32[]{:S(2)}, u32[]{:S(2)}) collective-permute-start(f32[64,128]{1,0:T(8,128)S(1)} %get-tuple-element.42), channel_id=1, source_target_pairs={{0,8},{8,0},{16,24},{24,16},{1,2},{9,10},{17,18},{25,26},{2,1},{10... | collective-permute-start | bytes 98312 | tf_op jit(solution)/shard_map/ppermute | solution.py:407
  51.2 5.4 %collective-permute-start.13 = (f32[64,128]{1,0:T(8,128)S(1)}, f32[64,128]{1,0:T(8,128)S(1)}, u32[]{:S(2)}, u32[]{:S(2)}) collective-permute-start(f32[64,128]{1,0:T(8,128)S(1)} %get-tuple-element.42), channel_id=1, source_target_pairs={{0,1},{1,0},{2,3},{3,2},{4,5},{5,4},{6,7},{7,6},{8,9},{9,8},{10,11... | collective-permute-start | bytes 98312 | tf_op jit(solution)/shard_map/ppermute | solution.py:385
  68.8 1.4 %collective-permute-start.15 = (f32[216,128]{1,0:T(8,128)S(1)}, f32[216,128]{1,0:T(8,128)S(1)}, u32[]{:S(2)}, u32[]{:S(2)}) collective-permute-start(f32[216,128]{1,0:T(8,128)S(1)} %get-tuple-element.44), channel_id=1, source_target_pairs={{0,4},{4,0},{1,5},{5,1},{2,6},{6,2},{3,7},{7,3},{8,12},{12,8},{9,1... | collective-permute-start | bytes 331784 | tf_op jit(solution)/shard_map/ppermute | solution.py:385
  70.2 4.1 %collective-permute-start.18 = (f32[88,128]{1,0:T(8,128)S(1)}, f32[88,128]{1,0:T(8,128)S(1)}, u32[]{:S(2)}, u32[]{:S(2)}) collective-permute-start(f32[88,128]{1,0:T(8,128)S(1)} %slice_add_fusion.2), channel_id=1, source_target_pairs={{0,16},{8,24},{16,0},{24,8},{1,17},{9,25},{17,1},{25,9},{2,18},{10... | collective-permute-start | bytes 135176 | tf_op jit(solution)/shard_map/ppermute | solution.py:385
  71.3 4.9 %collective-permute-start.17 = (f32[88,128]{1,0:T(8,128)S(1)}, f32[88,128]{1,0:T(8,128)S(1)}, u32[]{:S(2)}, u32[]{:S(2)}) collective-permute-start(f32[88,128]{1,0:T(8,128)S(1)} %slice_add_fusion.2), channel_id=1, source_target_pairs={{0,24},{8,16},{16,8},{24,0},{1,25},{9,17},{17,9},{25,1},{2,26},{10... | collective-permute-start | bytes 135176 | tf_op jit(solution)/shard_map/ppermute | solution.py:385
  72.7 4.0 %collective-permute-start.16 = (f32[88,128]{1,0:T(8,128)S(1)}, f32[88,128]{1,0:T(8,128)S(1)}, u32[]{:S(2)}, u32[]{:S(2)}) collective-permute-start(f32[88,128]{1,0:T(8,128)S(1)} %slice_add_fusion.2), channel_id=1, source_target_pairs={{0,8},{8,0},{16,24},{24,16},{1,9},{9,1},{17,25},{25,17},{2,10},{10... | collective-permute-start | bytes 135176 | tf_op jit(solution)/shard_map/ppermute | solution.py:385
  76.8 7.7 %collective-permute-start.20 = (f32[152,128]{1,0:T(8,128)S(1)}, f32[152,128]{1,0:T(8,128)S(1)}, u32[]{:S(2)}, u32[]{:S(2)}) collective-permute-start(f32[152,128]{1,0:T(8,128)S(1)} %constant_dynamic-update-slice_fusion.2), channel_id=1, source_target_pairs={{0,3},{1,2},{2,1},{3,0},{4,7},{5,6},{6,5},{7,4},{8,11},{9,10},{10,... | collective-permute-start | bytes 233480 | tf_op jit(solution)/shard_map/ppermute | solution.py:385
  78.7 6.6 %collective-permute-start.19 = (f32[152,128]{1,0:T(8,128)S(1)}, f32[152,128]{1,0:T(8,128)S(1)}, u32[]{:S(2)}, u32[]{:S(2)}) collective-permute-start(f32[152,128]{1,0:T(8,128)S(1)} %constant_dynamic-update-slice_fusion.2), channel_id=1, source_target_pairs={{0,1},{1,0},{2,3},{3,2},{4,5},{5,4},{6,7},{7,6},{8,9},{9,8},{10,11... | collective-permute-start | bytes 233480 | tf_op jit(solution)/shard_map/ppermute | solution.py:385
  79.4 5.1 %collective-permute-start.21 = (f32[88,128]{1,0:T(8,128)S(1)}, f32[88,128]{1,0:T(8,128)S(1)}, u32[]{:S(2)}, u32[]{:S(2)}) collective-permute-start(f32[88,128]{1,0:T(8,128)S(1)} %add_add_fusion), channel_id=1, source_target_pairs={{0,2},{1,3},{2,0},{3,1},{4,6},{5,7},{6,4},{7,5},{8,10},{9,11},{10,... | collective-permute-start | bytes 135176 | tf_op jit(solution)/shard_map/ppermute | solution.py:385
  81.2 5.4 %collective-permute-start.23 = (bf16[32,16,128]{2,1,0:T(8,128)(2,1)S(1)}, bf16[32,16,128]{2,1,0:T(8,128)(2,1)S(1)}, u32[]{:S(2)}, u32[]{:S(2)}) collective-permute-start(bf16[32,16,128]{2,1,0:T(8,128)(2,1)S(1)} %get-tuple-element.50), channel_id=1, source_target_pairs={{0,8},{8,0},{16,24},{24,16},{1,9},{9,1},{17,25},{25,17},{2,10},{10... | collective-permute-start | bytes 393224 | tf_op jit(solution)/shard_map/ppermute | solution.py:385
  82.3 5.0 %collective-permute-start.24 = (bf16[32,16,128]{2,1,0:T(8,128)(2,1)S(1)}, bf16[32,16,128]{2,1,0:T(8,128)(2,1)S(1)}, u32[]{:S(2)}, u32[]{:S(2)}) collective-permute-start(bf16[32,16,128]{2,1,0:T(8,128)(2,1)S(1)} %get-tuple-element.51), channel_id=1, source_target_pairs={{0,1},{1,0},{2,3},{3,2},{8,16},{9,17},{10,18},{11,19},{16,8},{17,9... | collective-permute-start | bytes 393224 | tf_op jit(solution)/shard_map/ppermute | solution.py:407
  85.3 1.3 %collective-permute-start.22 = (f32[88,128]{1,0:T(8,128)S(1)}, f32[88,128]{1,0:T(8,128)S(1)}, u32[]{:S(2)}, u32[]{:S(2)}) collective-permute-start(f32[88,128]{1,0:T(8,128)S(1)} %fusion.mine), channel_id=1, source_target_pairs={{0,4},{4,0},{1,5},{5,1},{2,6},{6,2},{3,7},{7,3},{8,12},{12,8},{9,1... | collective-permute-start | bytes 135176 | tf_op jit(solution)/shard_map/ppermute | solution.py:385

commit v2 on v1

--- a/solution.py
+++ b/solution.py
@@ -13,7 +13,7 @@
 PIVOTS = 8
 VOXEL_ROWS = 8
 CHUNK = 8
-TOGETHER = {"first": 4, "near": 8, "second": 4, "third": 8, "fourth": 4}
+TOGETHER = {"first": 8, "near": 8, "second": 8, "third": 8, "fourth": 4}
 f32, bf16 = jnp.float32, jnp.bfloat16
 
 

time: 100 us -> 99.4 us (level)
  no operation moved by 1% of the time
where the time goes in v2:
time: 99.4 us; the launch traced here: 99.2 us
  Pallas kernels  48.9 us (49%)
  starting transfers between devices  26.8 us (27%)
  waiting for transfers between devices  21.3 us (21%)
  local copies, waits for them, and re-layouts  1.33 us (1%)
    pallas_call x4, Pallas kernels, call(): pl.pallas_call(kernel, out_shape=tuple(outs), in_specs=specs, out_specs=t...  48.9 us
    ppermute x21, starting transfers between devices, send(): return lax.ppermute(value, axis, list(enumerate(to)))  23.3 us
    ppermute x21, waiting for transfers between devices, send(): return lax.ppermute(value, axis, list(enumerate(to)))  17.2 us
    ppermute x4, waiting for transfers between devices, send_middle(): return lax.ppermute(value, ('gx', 'gz'), pairs)  4.05 us
    ppermute x4, starting transfers between devices, send_middle(): return lax.ppermute(value, ('gx', 'gz'), pairs)  3.57 us
  transfers between devices with their start and end apart: 25, of which 17 were waited for; matrix products, arithmetic and copies ran while one was open for 0% of the time, Pallas kernels for 0%

profile of v2, /device:TPU:0, one launch (start us, length us, event | category | flops | bytes accessed | tf_op | source)
XLA Modules:
  0.0 99.2 jit_solution(16059268949135779321)
XLA Ops:
  0.7 0.1 stack.66.place
  0.8 0.0 copy-start
  0.8 1.2 %copy-done = bf16[16,8,32,128]{3,2,1,0:T(8,128)(2,1)S(1)} copy-done((bf16[16,8,32,128]{3,2,1,0:T(8,128)(2,1)S(1)}, bf16[16,8,32,128]{3,2,1,0:T(8,128)(2,1)}, u32[]{:S(2)}) %copy-start) | copy-done | bytes 1048600
  2.0 11.8 %shard_map.41 = (bf16[8,32,32,128]{3,2,1,0:T(8,128)(2,1)S(1)}, bf16[8,32,16,128]{3,2,1,0:T(8,128)(2,1)S(1)}, bf16[32,16,128]{2,1,0:T(8,128)(2,1)S(1)}, bf16[32,1...) custom-call(s32[12]{0:T(128)S(1)} %stack.66.place, ...), custom_call_target="tpu_custom_call" | custom-call | tf_op jit(solution)/shard_map/pallas_call | solution.py:454
  13.8 0.5 collective-permute-start
  14.3 1.0 collective-permute-done.yi.yo
  15.3 2.9 %collective-permute-start.3 = (f32[88,128]{1,0:T(8,128)S(1)}, f32[88,128]{1,0:T(8,128)S(1)}, u32[]{:S(2)}, u32[]{:S(2)}) collective-permute-start(f32[88,128]{1,0:T(8,128)S(1)} %slice_add_fusion.5), channel_id=1, source_target_pairs={{0,16},{8,24},{16,0},{24,8},{1,17},{9,25},{17,1},{25,9},{2,18},{10... | collective-permute-start | bytes 135176 | tf_op jit(solution)/shard_map/ppermute | solution.py:385
  18.2 1.4 %collective-permute-start.2 = (f32[88,128]{1,0:T(8,128)S(1)}, f32[88,128]{1,0:T(8,128)S(1)}, u32[]{:S(2)}, u32[]{:S(2)}) collective-permute-start(f32[88,128]{1,0:T(8,128)S(1)} %slice_add_fusion.5), channel_id=1, source_target_pairs={{0,24},{8,16},{16,8},{24,0},{1,25},{9,17},{17,9},{25,1},{2,26},{10... | collective-permute-start | bytes 135176 | tf_op jit(solution)/shard_map/ppermute | solution.py:385
  19.6 0.1 collective-permute-start.1
  19.7 0.5 collective-permute-done.3
  20.3 3.3 %collective-permute-done.2 = f32[88,128]{1,0:T(8,128)S(1)} collective-permute-done((f32[88,128]{1,0:T(8,128)S(1)}, f32[88,128]{1,0:T(8,128)S(1)}, u32[]{:S(2)}, u32[]{:S(2)}) %collective-permute-start.2) | collective-permute-done | bytes 45088 | tf_op jit(solution)/shard_map/ppermute | solution.py:385
  23.6 0.1 collective-permute-done.1
  23.7 3.7 %collective-permute-start.5 = (f32[152,128]{1,0:T(8,128)S(1)}, f32[152,128]{1,0:T(8,128)S(1)}, u32[]{:S(2)}, u32[]{:S(2)}) collective-permute-start(f32[152,128]{1,0:T(8,128)S(1)} %constant_dynamic-update-slice_fusion), channel_id=1, source_target_pairs={{0,3},{1,2},{2,1},{3,0},{4,7},{5,6},{6,5},{7,4},{8,11},{9,10},{10,... | collective-permute-start | bytes 233480 | tf_op jit(solution)/shard_map/ppermute | solution.py:385
  27.4 0.0 collective-permute-start.4
  27.4 0.8 collective-permute-start.6
  28.2 1.0 collective-permute-start.8
  29.1 1.2 %collective-permute-start.9 = (bf16[32,16,128]{2,1,0:T(8,128)(2,1)S(1)}, bf16[32,16,128]{2,1,0:T(8,128)(2,1)S(1)}, u32[]{:S(2)}, u32[]{:S(2)}) collective-permute-start(bf16[32,16,128]{2,1,0:T(8,128)(2,1)S(1)} %get-tuple-element.36), channel_id=1, source_target_pairs={{0,1},{1,0},{2,3},{3,2},{8,16},{9,17},{10,18},{11,19},{16,8},{17,9... | collective-permute-start | bytes 393224 | tf_op jit(solution)/shard_map/ppermute | solution.py:407
  30.4 2.1 %collective-permute-done.6 = f32[88,128]{1,0:T(8,128)S(1)} collective-permute-done((f32[88,128]{1,0:T(8,128)S(1)}, f32[88,128]{1,0:T(8,128)S(1)}, u32[]{:S(2)}, u32[]{:S(2)}) %collective-permute-start.6) | collective-permute-done | bytes 45088 | tf_op jit(solution)/shard_map/ppermute | solution.py:385
  32.4 0.0 collective-permute-done.5.zo
  32.4 0.7 collective-permute-done.4.zi
  33.2 0.1 collective-permute-start.7
  33.2 1.2 %collective-permute-done.7.theirs = f32[88,128]{1,0:T(8,128)S(1)} collective-permute-done((f32[88,128]{1,0:T(8,128)S(1)}, f32[88,128]{1,0:T(8,128)S(1)}, u32[]{:S(2)}, u32[]{:S(2)}) %collective-permute-start.7) | collective-permute-done | bytes 45088 | tf_op jit(solution)/shard_map/ppermute | solution.py:385
  34.5 0.0 collective-permute-done.8.xi
  34.5 0.6 collective-permute-done.9.xo
  35.1 12.2 %shard_map.42 = (f32[8,32,16,128]{3,2,1,0:T(8,128)S(1)}, bf16[8,32,16,128]{3,2,1,0:T(8,128)(2,1)S(1)}, bf16[32,16,128]{2,1,0:T(8,128)(2,1)S(1)}, bf16[32,16,128]...) custom-call(s32[12]{0:T(128)S(1)} %stack.66.place, ...), custom_call_target="tpu_custom_call" | custom-call | tf_op jit(solution)/shard_map/pallas_call | solution.py:454
  47.3 1.0 collective-permute-start.10
  48.3 1.4 %collective-permute-start.11 = (bf16[32,16,128]{2,1,0:T(8,128)(2,1)S(1)}, bf16[32,16,128]{2,1,0:T(8,128)(2,1)S(1)}, u32[]{:S(2)}, u32[]{:S(2)}) collective-permute-start(bf16[32,16,128]{2,1,0:T(8,128)(2,1)S(1)} %get-tuple-element.40), channel_id=1, source_target_pairs={{0,1},{1,0},{2,3},{3,2},{8,16},{9,17},{10,18},{11,19},{16,8},{17,9... | collective-permute-start | bytes 393224 | tf_op jit(solution)/shard_map/ppermute | solution.py:407
  49.6 0.0 collective-permute-start.12
  49.6 0.7 collective-permute-start.14
  50.4 2.6 %collective-permute-start.13 = (f32[64,128]{1,0:T(8,128)S(1)}, f32[64,128]{1,0:T(8,128)S(1)}, u32[]{:S(2)}, u32[]{:S(2)}) collective-permute-start(f32[64,128]{1,0:T(8,128)S(1)} %get-tuple-element.42), channel_id=1, source_target_pairs={{0,1},{1,0},{2,3},{3,2},{4,5},{5,4},{6,7},{7,6},{8,9},{9,8},{10,11... | collective-permute-start | bytes 98312 | tf_op jit(solution)/shard_map/ppermute | solution.py:385
  53.0 2.8 %collective-permute-done.14.zo = f32[64,128]{1,0:T(8,128)S(1)} collective-permute-done((f32[64,128]{1,0:T(8,128)S(1)}, f32[64,128]{1,0:T(8,128)S(1)}, u32[]{:S(2)}, u32[]{:S(2)}) %collective-permute-start.14) | collective-permute-done | bytes 32800 | tf_op jit(solution)/shard_map/ppermute | solution.py:407
  55.8 0.0 collective-permute-done.13.zi
  55.8 0.0 collective-permute-done.12.yi.yo
  55.8 0.0 collective-permute-done.10.xi
  55.8 0.0 collective-permute-done.11.xo
  55.8 12.4 %shard_map.43 = (bf16[8,32,16,128]{3,2,1,0:T(8,128)(2,1)S(1)}, bf16[32,16,128]{2,1,0:T(8,128)(2,1)S(1)}, bf16[32,16,128]{2,1,0:T(8,128)(2,1)S(1)}, f32[128,128]{...) custom-call(s32[12]{0:T(128)S(1)} %stack.66.place, ...), custom_call_target="tpu_custom_call" | custom-call | tf_op jit(solution)/shard_map/pallas_call | solution.py:454
  68.2 0.1 collective-permute-start.15
  68.2 1.3 %collective-permute-done.15.yi.yo = f32[216,128]{1,0:T(8,128)S(1)} collective-permute-done((f32[216,128]{1,0:T(8,128)S(1)}, f32[216,128]{1,0:T(8,128)S(1)}, u32[]{:S(2)}, u32[]{:S(2)}) %collective-permute-start.15) | collective-permute-done | bytes 110624 | tf_op jit(solution)/shard_map/ppermute | solution.py:385
  69.6 1.1 %collective-permute-start.18 = (f32[88,128]{1,0:T(8,128)S(1)}, f32[88,128]{1,0:T(8,128)S(1)}, u32[]{:S(2)}, u32[]{:S(2)}) collective-permute-start(f32[88,128]{1,0:T(8,128)S(1)} %slice_add_fusion.2), channel_id=1, source_target_pairs={{0,16},{8,24},{16,0},{24,8},{1,17},{9,25},{17,1},{25,9},{2,18},{10... | collective-permute-start | bytes 135176 | tf_op jit(solution)/shard_map/ppermute | solution.py:385
  70.7 1.4 %collective-permute-start.17 = (f32[88,128]{1,0:T(8,128)S(1)}, f32[88,128]{1,0:T(8,128)S(1)}, u32[]{:S(2)}, u32[]{:S(2)}) collective-permute-start(f32[88,128]{1,0:T(8,128)S(1)} %slice_add_fusion.2), channel_id=1, source_target_pairs={{0,24},{8,16},{16,8},{24,0},{1,25},{9,17},{17,9},{25,1},{2,26},{10... | collective-permute-start | bytes 135176 | tf_op jit(solution)/shard_map/ppermute | solution.py:385
  72.1 1.0 %collective-permute-start.16 = (f32[88,128]{1,0:T(8,128)S(1)}, f32[88,128]{1,0:T(8,128)S(1)}, u32[]{:S(2)}, u32[]{:S(2)}) collective-permute-start(f32[88,128]{1,0:T(8,128)S(1)} %slice_add_fusion.2), channel_id=1, source_target_pairs={{0,8},{8,0},{16,24},{24,16},{1,9},{9,1},{17,25},{25,17},{2,10},{10... | collective-permute-start | bytes 135176 | tf_op jit(solution)/shard_map/ppermute | solution.py:385
  73.1 0.6 collective-permute-done.18
  73.7 2.0 %collective-permute-done.17 = f32[88,128]{1,0:T(8,128)S(1)} collective-permute-done((f32[88,128]{1,0:T(8,128)S(1)}, f32[88,128]{1,0:T(8,128)S(1)}, u32[]{:S(2)}, u32[]{:S(2)}) %collective-permute-start.17) | collective-permute-done | bytes 45088 | tf_op jit(solution)/shard_map/ppermute | solution.py:385
  75.6 0.5 collective-permute-done.16
  76.2 1.9 %collective-permute-start.20 = (f32[152,128]{1,0:T(8,128)S(1)}, f32[152,128]{1,0:T(8,128)S(1)}, u32[]{:S(2)}, u32[]{:S(2)}) collective-permute-start(f32[152,128]{1,0:T(8,128)S(1)} %constant_dynamic-update-slice_fusion.2), channel_id=1, source_target_pairs={{0,3},{1,2},{2,1},{3,0},{4,7},{5,6},{6,5},{7,4},{8,11},{9,10},{10,... | collective-permute-start | bytes 233480 | tf_op jit(solution)/shard_map/ppermute | solution.py:385
  78.1 0.7 collective-permute-start.19
  78.8 1.8 %collective-permute-start.21 = (f32[88,128]{1,0:T(8,128)S(1)}, f32[88,128]{1,0:T(8,128)S(1)}, u32[]{:S(2)}, u32[]{:S(2)}) collective-permute-start(f32[88,128]{1,0:T(8,128)S(1)} %add_add_fusion), channel_id=1, source_target_pairs={{0,2},{1,3},{2,0},{3,1},{4,6},{5,7},{6,4},{7,5},{8,10},{9,11},{10,... | collective-permute-start | bytes 135176 | tf_op jit(solution)/shard_map/ppermute | solution.py:385
  80.6 1.0 %collective-permute-start.23 = (bf16[32,16,128]{2,1,0:T(8,128)(2,1)S(1)}, bf16[32,16,128]{2,1,0:T(8,128)(2,1)S(1)}, u32[]{:S(2)}, u32[]{:S(2)}) collective-permute-start(bf16[32,16,128]{2,1,0:T(8,128)(2,1)S(1)} %get-tuple-element.50), channel_id=1, source_target_pairs={{0,8},{8,0},{16,24},{24,16},{1,9},{9,1},{17,25},{25,17},{2,10},{10... | collective-permute-start | bytes 393224 | tf_op jit(solution)/shard_map/ppermute | solution.py:385
  81.6 0.2 collective-permute-start.24
  81.9 2.0 %collective-permute-done.21 = f32[88,128]{1,0:T(8,128)S(1)} collective-permute-done((f32[88,128]{1,0:T(8,128)S(1)}, f32[88,128]{1,0:T(8,128)S(1)}, u32[]{:S(2)}, u32[]{:S(2)}) %collective-permute-start.21) | collective-permute-done | bytes 45088 | tf_op jit(solution)/shard_map/ppermute | solution.py:385
  83.9 0.0 collective-permute-done.20.zo
  83.9 0.8 collective-permute-done.19.zi
  84.7 0.1 collective-permute-start.22
  84.8 1.2 %collective-permute-done.22.theirs = f32[88,128]{1,0:T(8,128)S(1)} collective-permute-done((f32[88,128]{1,0:T(8,128)S(1)}, f32[88,128]{1,0:T(8,128)S(1)}, u32[]{:S(2)}, u32[]{:S(2)}) %collective-permute-start.22) | collective-permute-done | bytes 45088 | tf_op jit(solution)/shard_map/ppermute | solution.py:385
  86.0 0.0 collective-permute-done.23.xi
  86.0 0.7 collective-permute-done.24.xo
  86.7 12.6 %shard_map.44 = (bf16[16,8,32,128]{3,2,1,0:T(8,128)(2,1)}, f32[16,32]{1,0:T(8,128)}) custom-call(s32[12]{0:T(128)S(1)} %stack.66.place, f32[88,128]{1,0:T(8,128)S(1)} %fusion.mine, f32[88,128]{1,0:T(8,128)S(1)} %collective-permute-done.22.theirs, bf16[8,32,32,128]{3,2,1,0:T(8,128)(2,1)S(1)} %get-tuple-element.33.xt, ...), custom_call_target="tpu_custom_call" | custom-call | tf_op jit(solution)/shard_map/pallas_call | solution.py:454
  (10 shorter events, 0.1 us)
Async XLA Ops:
  0.8 1.2 %copy-start = (bf16[16,8,32,128]{3,2,1,0:T(8,128)(2,1)S(1)}, bf16[16,8,32,128]{3,2,1,0:T(8,128)(2,1)}, u32[]{:S(2)}) copy-start(bf16[16,8,32,128]{3,2,1,0:T(8,128)(2,1)} %q_hbm.1) | copy-start | bytes 3145732
  13.8 1.5 %collective-permute-start = (f32[216,128]{1,0:T(8,128)S(1)}, f32[216,128]{1,0:T(8,128)S(1)}, u32[]{:S(2)}, u32[]{:S(2)}) collective-permute-start(f32[216,128]{1,0:T(8,128)S(1)} %get-tuple-element.28), channel_id=1, source_target_pairs={{0,4},{4,0},{1,5},{5,1},{2,6},{6,2},{3,7},{7,3},{8,12},{12,8},{9,1... | collective-permute-start | bytes 331784 | tf_op jit(solution)/shard_map/ppermute | solution.py:385
  15.3 5.0 %collective-permute-start.3 = (f32[88,128]{1,0:T(8,128)S(1)}, f32[88,128]{1,0:T(8,128)S(1)}, u32[]{:S(2)}, u32[]{:S(2)}) collective-permute-start(f32[88,128]{1,0:T(8,128)S(1)} %slice_add_fusion.5), channel_id=1, source_target_pairs={{0,16},{8,24},{16,0},{24,8},{1,17},{9,25},{17,1},{25,9},{2,18},{10... | collective-permute-start | bytes 135176 | tf_op jit(solution)/shard_map/ppermute | solution.py:385
  18.2 5.4 %collective-permute-start.2 = (f32[88,128]{1,0:T(8,128)S(1)}, f32[88,128]{1,0:T(8,128)S(1)}, u32[]{:S(2)}, u32[]{:S(2)}) collective-permute-start(f32[88,128]{1,0:T(8,128)S(1)} %slice_add_fusion.5), channel_id=1, source_target_pairs={{0,24},{8,16},{16,8},{24,0},{1,25},{9,17},{17,9},{25,1},{2,26},{10... | collective-permute-start | bytes 135176 | tf_op jit(solution)/shard_map/ppermute | solution.py:385
  19.6 4.0 %collective-permute-start.1 = (f32[88,128]{1,0:T(8,128)S(1)}, f32[88,128]{1,0:T(8,128)S(1)}, u32[]{:S(2)}, u32[]{:S(2)}) collective-permute-start(f32[88,128]{1,0:T(8,128)S(1)} %slice_add_fusion.5), channel_id=1, source_target_pairs={{0,8},{8,0},{16,24},{24,16},{1,9},{9,1},{17,25},{25,17},{2,10},{10... | collective-permute-start | bytes 135176 | tf_op jit(solution)/shard_map/ppermute | solution.py:385
  23.7 8.7 %collective-permute-start.5 = (f32[152,128]{1,0:T(8,128)S(1)}, f32[152,128]{1,0:T(8,128)S(1)}, u32[]{:S(2)}, u32[]{:S(2)}) collective-permute-start(f32[152,128]{1,0:T(8,128)S(1)} %constant_dynamic-update-slice_fusion), channel_id=1, source_target_pairs={{0,3},{1,2},{2,1},{3,0},{4,7},{5,6},{6,5},{7,4},{8,11},{9,10},{10,... | collective-permute-start | bytes 233480 | tf_op jit(solution)/shard_map/ppermute | solution.py:385
  27.4 5.8 %collective-permute-start.4 = (f32[152,128]{1,0:T(8,128)S(1)}, f32[152,128]{1,0:T(8,128)S(1)}, u32[]{:S(2)}, u32[]{:S(2)}) collective-permute-start(f32[152,128]{1,0:T(8,128)S(1)} %constant_dynamic-update-slice_fusion), channel_id=1, source_target_pairs={{0,1},{1,0},{2,3},{3,2},{4,5},{5,4},{6,7},{7,6},{8,9},{9,8},{10,11... | collective-permute-start | bytes 233480 | tf_op jit(solution)/shard_map/ppermute | solution.py:385
  27.4 5.1 %collective-permute-start.6 = (f32[88,128]{1,0:T(8,128)S(1)}, f32[88,128]{1,0:T(8,128)S(1)}, u32[]{:S(2)}, u32[]{:S(2)}) collective-permute-start(f32[88,128]{1,0:T(8,128)S(1)} %add_add_fusion.1), channel_id=1, source_target_pairs={{0,2},{1,3},{2,0},{3,1},{4,6},{5,7},{6,4},{7,5},{8,10},{9,11},{10,... | collective-permute-start | bytes 135176 | tf_op jit(solution)/shard_map/ppermute | solution.py:385
  28.2 6.3 %collective-permute-start.8 = (bf16[32,16,128]{2,1,0:T(8,128)(2,1)S(1)}, bf16[32,16,128]{2,1,0:T(8,128)(2,1)S(1)}, u32[]{:S(2)}, u32[]{:S(2)}) collective-permute-start(bf16[32,16,128]{2,1,0:T(8,128)(2,1)S(1)} %get-tuple-element.35), channel_id=1, source_target_pairs={{0,8},{8,0},{16,24},{24,16},{1,9},{9,1},{17,25},{25,17},{2,10},{10... | collective-permute-start | bytes 393224 | tf_op jit(solution)/shard_map/ppermute | solution.py:385
  29.1 5.9 %collective-permute-start.9 = (bf16[32,16,128]{2,1,0:T(8,128)(2,1)S(1)}, bf16[32,16,128]{2,1,0:T(8,128)(2,1)S(1)}, u32[]{:S(2)}, u32[]{:S(2)}) collective-permute-start(bf16[32,16,128]{2,1,0:T(8,128)(2,1)S(1)} %get-tuple-element.36), channel_id=1, source_target_pairs={{0,1},{1,0},{2,3},{3,2},{8,16},{9,17},{10,18},{11,19},{16,8},{17,9... | collective-permute-start | bytes 393224 | tf_op jit(solution)/shard_map/ppermute | solution.py:407
  33.2 1.3 %collective-permute-start.7 = (f32[88,128]{1,0:T(8,128)S(1)}, f32[88,128]{1,0:T(8,128)S(1)}, u32[]{:S(2)}, u32[]{:S(2)}) collective-permute-start(f32[88,128]{1,0:T(8,128)S(1)} %fusion.1.mine), channel_id=1, source_target_pairs={{0,4},{4,0},{1,5},{5,1},{2,6},{6,2},{3,7},{7,3},{8,12},{12,8},{9,1... | collective-permute-start | bytes 135176 | tf_op jit(solution)/shard_map/ppermute | solution.py:385
  47.3 8.5 %collective-permute-start.10 = (bf16[32,16,128]{2,1,0:T(8,128)(2,1)S(1)}, bf16[32,16,128]{2,1,0:T(8,128)(2,1)S(1)}, u32[]{:S(2)}, u32[]{:S(2)}) collective-permute-start(bf16[32,16,128]{2,1,0:T(8,128)(2,1)S(1)} %get-tuple-element.39), channel_id=1, source_target_pairs={{0,8},{8,0},{16,24},{24,16},{1,9},{9,1},{17,25},{25,17},{2,10},{10... | collective-permute-start | bytes 393224 | tf_op jit(solution)/shard_map/ppermute | solution.py:385
  48.3 7.5 %collective-permute-start.11 = (bf16[32,16,128]{2,1,0:T(8,128)(2,1)S(1)}, bf16[32,16,128]{2,1,0:T(8,128)(2,1)S(1)}, u32[]{:S(2)}, u32[]{:S(2)}) collective-permute-start(bf16[32,16,128]{2,1,0:T(8,128)(2,1)S(1)} %get-tuple-element.40), channel_id=1, source_target_pairs={{0,1},{1,0},{2,3},{3,2},{8,16},{9,17},{10,18},{11,19},{16,8},{17,9... | collective-permute-start | bytes 393224 | tf_op jit(solution)/shard_map/ppermute | solution.py:407
  49.6 6.1 %collective-permute-start.12 = (f32[128,128]{1,0:T(8,128)S(1)}, f32[128,128]{1,0:T(8,128)S(1)}, u32[]{:S(2)}, u32[]{:S(2)}) collective-permute-start(f32[128,128]{1,0:T(8,128)S(1)} %get-tuple-element.41), channel_id=1, source_target_pairs={{0,4},{4,0},{1,5},{5,1},{2,6},{6,2},{3,7},{7,3},{8,12},{12,8},{9,1... | collective-permute-start | bytes 196616 | tf_op jit(solution)/shard_map/ppermute | solution.py:385
  49.6 6.1 %collective-permute-start.14 = (f32[64,128]{1,0:T(8,128)S(1)}, f32[64,128]{1,0:T(8,128)S(1)}, u32[]{:S(2)}, u32[]{:S(2)}) collective-permute-start(f32[64,128]{1,0:T(8,128)S(1)} %get-tuple-element.42), channel_id=1, source_target_pairs={{0,8},{8,0},{16,24},{24,16},{1,2},{9,10},{17,18},{25,26},{2,1},{10... | collective-permute-start | bytes 98312 | tf_op jit(solution)/shard_map/ppermute | solution.py:407
  50.4 5.4 %collective-permute-start.13 = (f32[64,128]{1,0:T(8,128)S(1)}, f32[64,128]{1,0:T(8,128)S(1)}, u32[]{:S(2)}, u32[]{:S(2)}) collective-permute-start(f32[64,128]{1,0:T(8,128)S(1)} %get-tuple-element.42), channel_id=1, source_target_pairs={{0,1},{1,0},{2,3},{3,2},{4,5},{5,4},{6,7},{7,6},{8,9},{9,8},{10,11... | collective-permute-start | bytes 98312 | tf_op jit(solution)/shard_map/ppermute | solution.py:385
  68.2 1.4 %collective-permute-start.15 = (f32[216,128]{1,0:T(8,128)S(1)}, f32[216,128]{1,0:T(8,128)S(1)}, u32[]{:S(2)}, u32[]{:S(2)}) collective-permute-start(f32[216,128]{1,0:T(8,128)S(1)} %get-tuple-element.44), channel_id=1, source_target_pairs={{0,4},{4,0},{1,5},{5,1},{2,6},{6,2},{3,7},{7,3},{8,12},{12,8},{9,1... | collective-permute-start | bytes 331784 | tf_op jit(solution)/shard_map/ppermute | solution.py:385
  69.6 4.1 %collective-permute-start.18 = (f32[88,128]{1,0:T(8,128)S(1)}, f32[88,128]{1,0:T(8,128)S(1)}, u32[]{:S(2)}, u32[]{:S(2)}) collective-permute-start(f32[88,128]{1,0:T(8,128)S(1)} %slice_add_fusion.2), channel_id=1, source_target_pairs={{0,16},{8,24},{16,0},{24,8},{1,17},{9,25},{17,1},{25,9},{2,18},{10... | collective-permute-start | bytes 135176 | tf_op jit(solution)/shard_map/ppermute | solution.py:385
  70.7 4.9 %collective-permute-start.17 = (f32[88,128]{1,0:T(8,128)S(1)}, f32[88,128]{1,0:T(8,128)S(1)}, u32[]{:S(2)}, u32[]{:S(2)}) collective-permute-start(f32[88,128]{1,0:T(8,128)S(1)} %slice_add_fusion.2), channel_id=1, source_target_pairs={{0,24},{8,16},{16,8},{24,0},{1,25},{9,17},{17,9},{25,1},{2,26},{10... | collective-permute-start | bytes 135176 | tf_op jit(solution)/shard_map/ppermute | solution.py:385
  72.1 4.0 %collective-permute-start.16 = (f32[88,128]{1,0:T(8,128)S(1)}, f32[88,128]{1,0:T(8,128)S(1)}, u32[]{:S(2)}, u32[]{:S(2)}) collective-permute-start(f32[88,128]{1,0:T(8,128)S(1)} %slice_add_fusion.2), channel_id=1, source_target_pairs={{0,8},{8,0},{16,24},{24,16},{1,9},{9,1},{17,25},{25,17},{2,10},{10... | collective-permute-start | bytes 135176 | tf_op jit(solution)/shard_map/ppermute | solution.py:385
  76.2 7.7 %collective-permute-start.20 = (f32[152,128]{1,0:T(8,128)S(1)}, f32[152,128]{1,0:T(8,128)S(1)}, u32[]{:S(2)}, u32[]{:S(2)}) collective-permute-start(f32[152,128]{1,0:T(8,128)S(1)} %constant_dynamic-update-slice_fusion.2), channel_id=1, source_target_pairs={{0,3},{1,2},{2,1},{3,0},{4,7},{5,6},{6,5},{7,4},{8,11},{9,10},{10,... | collective-permute-start | bytes 233480 | tf_op jit(solution)/shard_map/ppermute | solution.py:385
  78.1 6.6 %collective-permute-start.19 = (f32[152,128]{1,0:T(8,128)S(1)}, f32[152,128]{1,0:T(8,128)S(1)}, u32[]{:S(2)}, u32[]{:S(2)}) collective-permute-start(f32[152,128]{1,0:T(8,128)S(1)} %constant_dynamic-update-slice_fusion.2), channel_id=1, source_target_pairs={{0,1},{1,0},{2,3},{3,2},{4,5},{5,4},{6,7},{7,6},{8,9},{9,8},{10,11... | collective-permute-start | bytes 233480 | tf_op jit(solution)/shard_map/ppermute | solution.py:385
  78.8 5.1 %collective-permute-start.21 = (f32[88,128]{1,0:T(8,128)S(1)}, f32[88,128]{1,0:T(8,128)S(1)}, u32[]{:S(2)}, u32[]{:S(2)}) collective-permute-start(f32[88,128]{1,0:T(8,128)S(1)} %add_add_fusion), channel_id=1, source_target_pairs={{0,2},{1,3},{2,0},{3,1},{4,6},{5,7},{6,4},{7,5},{8,10},{9,11},{10,... | collective-permute-start | bytes 135176 | tf_op jit(solution)/shard_map/ppermute | solution.py:385
  80.6 5.4 %collective-permute-start.23 = (bf16[32,16,128]{2,1,0:T(8,128)(2,1)S(1)}, bf16[32,16,128]{2,1,0:T(8,128)(2,1)S(1)}, u32[]{:S(2)}, u32[]{:S(2)}) collective-permute-start(bf16[32,16,128]{2,1,0:T(8,128)(2,1)S(1)} %get-tuple-element.50), channel_id=1, source_target_pairs={{0,8},{8,0},{16,24},{24,16},{1,9},{9,1},{17,25},{25,17},{2,10},{10... | collective-permute-start | bytes 393224 | tf_op jit(solution)/shard_map/ppermute | solution.py:385
  81.6 5.0 %collective-permute-start.24 = (bf16[32,16,128]{2,1,0:T(8,128)(2,1)S(1)}, bf16[32,16,128]{2,1,0:T(8,128)(2,1)S(1)}, u32[]{:S(2)}, u32[]{:S(2)}) collective-permute-start(bf16[32,16,128]{2,1,0:T(8,128)(2,1)S(1)} %get-tuple-element.51), channel_id=1, source_target_pairs={{0,1},{1,0},{2,3},{3,2},{8,16},{9,17},{10,18},{11,19},{16,8},{17,9... | collective-permute-start | bytes 393224 | tf_op jit(solution)/shard_map/ppermute | solution.py:407
  84.7 1.3 %collective-permute-start.22 = (f32[88,128]{1,0:T(8,128)S(1)}, f32[88,128]{1,0:T(8,128)S(1)}, u32[]{:S(2)}, u32[]{:S(2)}) collective-permute-start(f32[88,128]{1,0:T(8,128)S(1)} %fusion.mine), channel_id=1, source_target_pairs={{0,4},{4,0},{1,5},{5,1},{2,6},{6,2},{3,7},{7,3},{8,12},{12,8},{9,1... | collective-permute-start | bytes 135176 | tf_op jit(solution)/shard_map/ppermute | solution.py:385

commit v3 on v2

--- a/solution.py
+++ b/solution.py
@@ -22,7 +22,7 @@
 
 
 def half_rows(feats, classes):
-    return -(-(feats * feats * classes // 128 + feats + 8) // 16) * 8
+    return -(-(feats * feats * classes // 128 + feats) // 16) * 8
 
 
 def moments_of(x, q):
@@ -53,12 +53,17 @@
 
 def put_moments(place_ref, mine, theirs, scatter, rest):
     feats, lanes = scatter.shape
+    classes = rest.shape[0] - 128
     rows = [scatter[:, j : j + 128] for j in range(0, lanes, 128)]
     rest = jnp.pad(rest, ((0, 256 - rest.shape[0]), (0, 128 - rest.shape[1])))
     rows.append(rest[:128].T[:feats])
-    rows.append(rest[128:].T[: feats + 8])
+    first = rest[128:].T
+    counts = pltpu.roll(first[feats : feats + 8], classes, 1)[:1]
+    rows.append(first[:feats] + jnp.where(iota((feats, 128), 0) == 0, counts, 0.0))
     half = mine.shape[0]
-    rows.append(jnp.zeros((2 * half - sum(r.shape[0] for r in rows), 128), f32))
+    spare = 2 * half - sum(r.shape[0] for r in rows)
+    if spare:
+        rows.append(jnp.zeros((spare, 128), f32))
     rows = jnp.concatenate(rows, axis=0)
     odd = Place(place_ref, 1).sends == 1
     mine[...] = jnp.where(odd, rows[half:], rows[:half])
@@ -89,7 +94,7 @@
         return jnp.broadcast_to(v[r : r + 1], (8, 128))
 
     base = tiles * feats
-    counts = spread_lanes(spread_row(rows(base + feats), 0), 0)
+    counts = spread_lanes(spread_row(rows(base), 0), 1)
     inv = 1.0 / counts
     means = [spread_lanes(rows(base + 8 * j), 0) / counts for j in range(tiles)]
     eye = jnp.where(sub == group, 1.0, 0.0)

time: 99.4 us -> 99.3 us (level)
  waiting for transfers between devices: 21.3 us -> 20.3 us
where the time goes in v3:
time: 99.3 us; the launch traced here: 99.1 us
  Pallas kernels  49.3 us (50%)
  starting transfers between devices  27.3 us (27%)
  waiting for transfers between devices  20.3 us (20%)
  local copies, waits for them, and re-layouts  1.33 us (1%)
    pallas_call x4, Pallas kernels, call(): pl.pallas_call(kernel, out_shape=tuple(outs), in_specs=specs, out_specs=t...  49.3 us
    ppermute x21, starting transfers between devices, send(): return lax.ppermute(value, axis, list(enumerate(to)))  23.6 us
    ppermute x21, waiting for transfers between devices, send(): return lax.ppermute(value, axis, list(enumerate(to)))  16.6 us
    ppermute x4, starting transfers between devices, send_middle(): return lax.ppermute(value, ('gx', 'gz'), pairs)  3.72 us
    ppermute x4, waiting for transfers between devices, send_middle(): return lax.ppermute(value, ('gx', 'gz'), pairs)  3.68 us
  transfers between devices with their start and end apart: 25, of which 17 were waited for; matrix products, arithmetic and copies ran while one was open for 0% of the time, Pallas kernels for 0%

profile of v3, /device:TPU:0, one launch (start us, length us, event | category | flops | bytes accessed | tf_op | source)
XLA Modules:
  0.0 99.1 jit_solution(13731404098318305923)
XLA Ops:
  0.7 0.1 stack.66.place
  0.8 0.0 copy-start
  0.8 1.2 %copy-done = bf16[16,8,32,128]{3,2,1,0:T(8,128)(2,1)S(1)} copy-done((bf16[16,8,32,128]{3,2,1,0:T(8,128)(2,1)S(1)}, bf16[16,8,32,128]{3,2,1,0:T(8,128)(2,1)}, u32[]{:S(2)}) %copy-start) | copy-done | bytes 1048600
  2.0 11.8 %shard_map.41 = (bf16[8,32,32,128]{3,2,1,0:T(8,128)(2,1)S(1)}, bf16[8,32,16,128]{3,2,1,0:T(8,128)(2,1)S(1)}, bf16[32,16,128]{2,1,0:T(8,128)(2,1)S(1)}, bf16[32,1...) custom-call(s32[12]{0:T(128)S(1)} %stack.66.place, ...), custom_call_target="tpu_custom_call" | custom-call | tf_op jit(solution)/shard_map/pallas_call | solution.py:459
  13.8 0.5 collective-permute-start
  14.3 1.0 collective-permute-done.yi.yo
  15.3 2.9 %collective-permute-start.3 = (f32[80,128]{1,0:T(8,128)S(1)}, f32[80,128]{1,0:T(8,128)S(1)}, u32[]{:S(2)}, u32[]{:S(2)}) collective-permute-start(f32[80,128]{1,0:T(8,128)S(1)} %slice_add_fusion.5), channel_id=1, source_target_pairs={{0,16},{8,24},{16,0},{24,8},{1,17},{9,25},{17,1},{25,9},{2,18},{10... | collective-permute-start | bytes 122888 | tf_op jit(solution)/shard_map/ppermute | solution.py:390
  18.1 1.4 %collective-permute-start.2 = (f32[80,128]{1,0:T(8,128)S(1)}, f32[80,128]{1,0:T(8,128)S(1)}, u32[]{:S(2)}, u32[]{:S(2)}) collective-permute-start(f32[80,128]{1,0:T(8,128)S(1)} %slice_add_fusion.5), channel_id=1, source_target_pairs={{0,24},{8,16},{16,8},{24,0},{1,25},{9,17},{17,9},{25,1},{2,26},{10... | collective-permute-start | bytes 122888 | tf_op jit(solution)/shard_map/ppermute | solution.py:390
  19.6 0.1 collective-permute-start.1
  19.7 0.4 collective-permute-done.3
  20.1 3.2 %collective-permute-done.2 = f32[80,128]{1,0:T(8,128)S(1)} collective-permute-done((f32[80,128]{1,0:T(8,128)S(1)}, f32[80,128]{1,0:T(8,128)S(1)}, u32[]{:S(2)}, u32[]{:S(2)}) %collective-permute-start.2) | collective-permute-done | bytes 40992 | tf_op jit(solution)/shard_map/ppermute | solution.py:390
  23.3 0.2 collective-permute-done.1
  23.6 3.7 %collective-permute-start.5 = (f32[144,128]{1,0:T(8,128)S(1)}, f32[144,128]{1,0:T(8,128)S(1)}, u32[]{:S(2)}, u32[]{:S(2)}) collective-permute-start(f32[144,128]{1,0:T(8,128)S(1)} %constant_dynamic-update-slice_fusion), channel_id=1, source_target_pairs={{0,3},{1,2},{2,1},{3,0},{4,7},{5,6},{6,5},{7,4},{8,11},{9,10},{10,... | collective-permute-start | bytes 221192 | tf_op jit(solution)/shard_map/ppermute | solution.py:390
  27.3 0.0 collective-permute-start.4
  27.3 0.8 collective-permute-start.6
  28.1 1.0 collective-permute-start.8
  29.0 1.2 %collective-permute-start.9 = (bf16[32,16,128]{2,1,0:T(8,128)(2,1)S(1)}, bf16[32,16,128]{2,1,0:T(8,128)(2,1)S(1)}, u32[]{:S(2)}, u32[]{:S(2)}) collective-permute-start(bf16[32,16,128]{2,1,0:T(8,128)(2,1)S(1)} %get-tuple-element.36), channel_id=1, source_target_pairs={{0,1},{1,0},{2,3},{3,2},{8,16},{9,17},{10,18},{11,19},{16,8},{17,9... | collective-permute-start | bytes 393224 | tf_op jit(solution)/shard_map/ppermute | solution.py:412
  30.3 2.0 %collective-permute-done.6 = f32[80,128]{1,0:T(8,128)S(1)} collective-permute-done((f32[80,128]{1,0:T(8,128)S(1)}, f32[80,128]{1,0:T(8,128)S(1)}, u32[]{:S(2)}, u32[]{:S(2)}) %collective-permute-start.6) | collective-permute-done | bytes 40992 | tf_op jit(solution)/shard_map/ppermute | solution.py:390
  32.3 0.0 collective-permute-done.5.zo
  32.3 0.6 collective-permute-done.4.zi
  32.9 0.1 collective-permute-start.7
  33.0 1.2 %collective-permute-done.7.theirs = f32[80,128]{1,0:T(8,128)S(1)} collective-permute-done((f32[80,128]{1,0:T(8,128)S(1)}, f32[80,128]{1,0:T(8,128)S(1)}, u32[]{:S(2)}, u32[]{:S(2)}) %collective-permute-start.7) | collective-permute-done | bytes 40992 | tf_op jit(solution)/shard_map/ppermute | solution.py:390
  34.2 0.0 collective-permute-done.8.xi
  34.2 0.2 collective-permute-done.9.xo
  34.4 12.2 %shard_map.42 = (f32[8,32,16,128]{3,2,1,0:T(8,128)S(1)}, bf16[8,32,16,128]{3,2,1,0:T(8,128)(2,1)S(1)}, bf16[32,16,128]{2,1,0:T(8,128)(2,1)S(1)}, bf16[32,16,128]...) custom-call(s32[12]{0:T(128)S(1)} %stack.66.place, ...), custom_call_target="tpu_custom_call" | custom-call | tf_op jit(solution)/shard_map/pallas_call | solution.py:459
  46.6 1.6 %collective-permute-start.10 = (bf16[32,16,128]{2,1,0:T(8,128)(2,1)S(1)}, bf16[32,16,128]{2,1,0:T(8,128)(2,1)S(1)}, u32[]{:S(2)}, u32[]{:S(2)}) collective-permute-start(bf16[32,16,128]{2,1,0:T(8,128)(2,1)S(1)} %get-tuple-element.39), channel_id=1, source_target_pairs={{0,8},{8,0},{16,24},{24,16},{1,9},{9,1},{17,25},{25,17},{2,10},{10... | collective-permute-start | bytes 393224 | tf_op jit(solution)/shard_map/ppermute | solution.py:390
  48.1 1.2 %collective-permute-start.11 = (bf16[32,16,128]{2,1,0:T(8,128)(2,1)S(1)}, bf16[32,16,128]{2,1,0:T(8,128)(2,1)S(1)}, u32[]{:S(2)}, u32[]{:S(2)}) collective-permute-start(bf16[32,16,128]{2,1,0:T(8,128)(2,1)S(1)} %get-tuple-element.40), channel_id=1, source_target_pairs={{0,1},{1,0},{2,3},{3,2},{8,16},{9,17},{10,18},{11,19},{16,8},{17,9... | collective-permute-start | bytes 393224 | tf_op jit(solution)/shard_map/ppermute | solution.py:412
  49.4 0.0 collective-permute-start.12
  49.4 0.8 collective-permute-start.14
  50.2 2.6 %collective-permute-start.13 = (f32[64,128]{1,0:T(8,128)S(1)}, f32[64,128]{1,0:T(8,128)S(1)}, u32[]{:S(2)}, u32[]{:S(2)}) collective-permute-start(f32[64,128]{1,0:T(8,128)S(1)} %get-tuple-element.42), channel_id=1, source_target_pairs={{0,1},{1,0},{2,3},{3,2},{4,5},{5,4},{6,7},{7,6},{8,9},{9,8},{10,11... | collective-permute-start | bytes 98312 | tf_op jit(solution)/shard_map/ppermute | solution.py:390
  52.9 2.6 %collective-permute-done.14.zo = f32[64,128]{1,0:T(8,128)S(1)} collective-permute-done((f32[64,128]{1,0:T(8,128)S(1)}, f32[64,128]{1,0:T(8,128)S(1)}, u32[]{:S(2)}, u32[]{:S(2)}) %collective-permute-start.14) | collective-permute-done | bytes 32800 | tf_op jit(solution)/shard_map/ppermute | solution.py:412
  55.5 0.0 collective-permute-done.13.zi
  55.5 0.0 collective-permute-done.12.yi.yo
  55.5 0.0 collective-permute-done.10.xi
  55.5 0.0 collective-permute-done.11.xo
  55.5 12.8 %shard_map.43 = (bf16[8,32,16,128]{3,2,1,0:T(8,128)(2,1)S(1)}, bf16[32,16,128]{2,1,0:T(8,128)(2,1)S(1)}, bf16[32,16,128]{2,1,0:T(8,128)(2,1)S(1)}, f32[128,128]{...) custom-call(s32[12]{0:T(128)S(1)} %stack.66.place, ...), custom_call_target="tpu_custom_call" | custom-call | tf_op jit(solution)/shard_map/pallas_call | solution.py:459
  68.3 0.0 collective-permute-start.15
  68.3 1.3 %collective-permute-done.15.yi.yo = f32[208,128]{1,0:T(8,128)S(1)} collective-permute-done((f32[208,128]{1,0:T(8,128)S(1)}, f32[208,128]{1,0:T(8,128)S(1)}, u32[]{:S(2)}, u32[]{:S(2)}) %collective-permute-start.15) | collective-permute-done | bytes 106528 | tf_op jit(solution)/shard_map/ppermute | solution.py:390
  69.6 1.1 %collective-permute-start.18 = (f32[80,128]{1,0:T(8,128)S(1)}, f32[80,128]{1,0:T(8,128)S(1)}, u32[]{:S(2)}, u32[]{:S(2)}) collective-permute-start(f32[80,128]{1,0:T(8,128)S(1)} %slice_add_fusion.2), channel_id=1, source_target_pairs={{0,16},{8,24},{16,0},{24,8},{1,17},{9,25},{17,1},{25,9},{2,18},{10... | collective-permute-start | bytes 122888 | tf_op jit(solution)/shard_map/ppermute | solution.py:390
  70.7 1.4 %collective-permute-start.17 = (f32[80,128]{1,0:T(8,128)S(1)}, f32[80,128]{1,0:T(8,128)S(1)}, u32[]{:S(2)}, u32[]{:S(2)}) collective-permute-start(f32[80,128]{1,0:T(8,128)S(1)} %slice_add_fusion.2), channel_id=1, source_target_pairs={{0,24},{8,16},{16,8},{24,0},{1,25},{9,17},{17,9},{25,1},{2,26},{10... | collective-permute-start | bytes 122888 | tf_op jit(solution)/shard_map/ppermute | solution.py:390
  72.1 1.0 %collective-permute-start.16 = (f32[80,128]{1,0:T(8,128)S(1)}, f32[80,128]{1,0:T(8,128)S(1)}, u32[]{:S(2)}, u32[]{:S(2)}) collective-permute-start(f32[80,128]{1,0:T(8,128)S(1)} %slice_add_fusion.2), channel_id=1, source_target_pairs={{0,8},{8,0},{16,24},{24,16},{1,9},{9,1},{17,25},{25,17},{2,10},{10... | collective-permute-start | bytes 122888 | tf_op jit(solution)/shard_map/ppermute | solution.py:390
  73.1 0.5 collective-permute-done.18
  73.6 2.0 %collective-permute-done.17 = f32[80,128]{1,0:T(8,128)S(1)} collective-permute-done((f32[80,128]{1,0:T(8,128)S(1)}, f32[80,128]{1,0:T(8,128)S(1)}, u32[]{:S(2)}, u32[]{:S(2)}) %collective-permute-start.17) | collective-permute-done | bytes 40992 | tf_op jit(solution)/shard_map/ppermute | solution.py:390
  75.6 0.5 collective-permute-done.16
  76.1 2.1 %collective-permute-start.20 = (f32[144,128]{1,0:T(8,128)S(1)}, f32[144,128]{1,0:T(8,128)S(1)}, u32[]{:S(2)}, u32[]{:S(2)}) collective-permute-start(f32[144,128]{1,0:T(8,128)S(1)} %constant_dynamic-update-slice_fusion.2), channel_id=1, source_target_pairs={{0,3},{1,2},{2,1},{3,0},{4,7},{5,6},{6,5},{7,4},{8,11},{9,10},{10,... | collective-permute-start | bytes 221192 | tf_op jit(solution)/shard_map/ppermute | solution.py:390
  78.2 0.6 collective-permute-start.19
  78.8 1.8 %collective-permute-start.21 = (f32[80,128]{1,0:T(8,128)S(1)}, f32[80,128]{1,0:T(8,128)S(1)}, u32[]{:S(2)}, u32[]{:S(2)}) collective-permute-start(f32[80,128]{1,0:T(8,128)S(1)} %add_add_fusion), channel_id=1, source_target_pairs={{0,2},{1,3},{2,0},{3,1},{4,6},{5,7},{6,4},{7,5},{8,10},{9,11},{10,... | collective-permute-start | bytes 122888 | tf_op jit(solution)/shard_map/ppermute | solution.py:390
  80.6 1.0 %collective-permute-start.23 = (bf16[32,16,128]{2,1,0:T(8,128)(2,1)S(1)}, bf16[32,16,128]{2,1,0:T(8,128)(2,1)S(1)}, u32[]{:S(2)}, u32[]{:S(2)}) collective-permute-start(bf16[32,16,128]{2,1,0:T(8,128)(2,1)S(1)} %get-tuple-element.50), channel_id=1, source_target_pairs={{0,8},{8,0},{16,24},{24,16},{1,9},{9,1},{17,25},{25,17},{2,10},{10... | collective-permute-start | bytes 393224 | tf_op jit(solution)/shard_map/ppermute | solution.py:390
  81.6 0.4 collective-permute-start.24
  82.0 1.8 %collective-permute-done.21 = f32[80,128]{1,0:T(8,128)S(1)} collective-permute-done((f32[80,128]{1,0:T(8,128)S(1)}, f32[80,128]{1,0:T(8,128)S(1)}, u32[]{:S(2)}, u32[]{:S(2)}) %collective-permute-start.21) | collective-permute-done | bytes 40992 | tf_op jit(solution)/shard_map/ppermute | solution.py:390
  83.8 0.0 collective-permute-done.20.zo
  83.8 0.6 collective-permute-done.19.zi
  84.4 0.1 collective-permute-start.22
  84.5 1.2 %collective-permute-done.22.theirs = f32[80,128]{1,0:T(8,128)S(1)} collective-permute-done((f32[80,128]{1,0:T(8,128)S(1)}, f32[80,128]{1,0:T(8,128)S(1)}, u32[]{:S(2)}, u32[]{:S(2)}) %collective-permute-start.22) | collective-permute-done | bytes 40992 | tf_op jit(solution)/shard_map/ppermute | solution.py:390
  85.7 0.0 collective-permute-done.23.xi
  85.7 0.9 collective-permute-done.24.xo
  86.6 12.5 %shard_map.44 = (bf16[16,8,32,128]{3,2,1,0:T(8,128)(2,1)}, f32[16,32]{1,0:T(8,128)}) custom-call(s32[12]{0:T(128)S(1)} %stack.66.place, f32[80,128]{1,0:T(8,128)S(1)} %fusion.mine, f32[80,128]{1,0:T(8,128)S(1)} %collective-permute-done.22.theirs, bf16[8,32,32,128]{3,2,1,0:T(8,128)(2,1)S(1)} %get-tuple-element.33.xt, ...), custom_call_target="tpu_custom_call" | custom-call | tf_op jit(solution)/shard_map/pallas_call | solution.py:459
  (10 shorter events, 0.1 us)
Async XLA Ops:
  0.8 1.2 %copy-start = (bf16[16,8,32,128]{3,2,1,0:T(8,128)(2,1)S(1)}, bf16[16,8,32,128]{3,2,1,0:T(8,128)(2,1)}, u32[]{:S(2)}) copy-start(bf16[16,8,32,128]{3,2,1,0:T(8,128)(2,1)} %q_hbm.1) | copy-start | bytes 3145732
  13.8 1.5 %collective-permute-start = (f32[208,128]{1,0:T(8,128)S(1)}, f32[208,128]{1,0:T(8,128)S(1)}, u32[]{:S(2)}, u32[]{:S(2)}) collective-permute-start(f32[208,128]{1,0:T(8,128)S(1)} %get-tuple-element.28), channel_id=1, source_target_pairs={{0,4},{4,0},{1,5},{5,1},{2,6},{6,2},{3,7},{7,3},{8,12},{12,8},{9,1... | collective-permute-start | bytes 319496 | tf_op jit(solution)/shard_map/ppermute | solution.py:390
  15.3 4.9 %collective-permute-start.3 = (f32[80,128]{1,0:T(8,128)S(1)}, f32[80,128]{1,0:T(8,128)S(1)}, u32[]{:S(2)}, u32[]{:S(2)}) collective-permute-start(f32[80,128]{1,0:T(8,128)S(1)} %slice_add_fusion.5), channel_id=1, source_target_pairs={{0,16},{8,24},{16,0},{24,8},{1,17},{9,25},{17,1},{25,9},{2,18},{10... | collective-permute-start | bytes 122888 | tf_op jit(solution)/shard_map/ppermute | solution.py:390
  18.1 5.2 %collective-permute-start.2 = (f32[80,128]{1,0:T(8,128)S(1)}, f32[80,128]{1,0:T(8,128)S(1)}, u32[]{:S(2)}, u32[]{:S(2)}) collective-permute-start(f32[80,128]{1,0:T(8,128)S(1)} %slice_add_fusion.5), channel_id=1, source_target_pairs={{0,24},{8,16},{16,8},{24,0},{1,25},{9,17},{17,9},{25,1},{2,26},{10... | collective-permute-start | bytes 122888 | tf_op jit(solution)/shard_map/ppermute | solution.py:390
  19.6 4.0 %collective-permute-start.1 = (f32[80,128]{1,0:T(8,128)S(1)}, f32[80,128]{1,0:T(8,128)S(1)}, u32[]{:S(2)}, u32[]{:S(2)}) collective-permute-start(f32[80,128]{1,0:T(8,128)S(1)} %slice_add_fusion.5), channel_id=1, source_target_pairs={{0,8},{8,0},{16,24},{24,16},{1,9},{9,1},{17,25},{25,17},{2,10},{10... | collective-permute-start | bytes 122888 | tf_op jit(solution)/shard_map/ppermute | solution.py:390
  23.6 8.7 %collective-permute-start.5 = (f32[144,128]{1,0:T(8,128)S(1)}, f32[144,128]{1,0:T(8,128)S(1)}, u32[]{:S(2)}, u32[]{:S(2)}) collective-permute-start(f32[144,128]{1,0:T(8,128)S(1)} %constant_dynamic-update-slice_fusion), channel_id=1, source_target_pairs={{0,3},{1,2},{2,1},{3,0},{4,7},{5,6},{6,5},{7,4},{8,11},{9,10},{10,... | collective-permute-start | bytes 221192 | tf_op jit(solution)/shard_map/ppermute | solution.py:390
  27.3 5.6 %collective-permute-start.4 = (f32[144,128]{1,0:T(8,128)S(1)}, f32[144,128]{1,0:T(8,128)S(1)}, u32[]{:S(2)}, u32[]{:S(2)}) collective-permute-start(f32[144,128]{1,0:T(8,128)S(1)} %constant_dynamic-update-slice_fusion), channel_id=1, source_target_pairs={{0,1},{1,0},{2,3},{3,2},{4,5},{5,4},{6,7},{7,6},{8,9},{9,8},{10,11... | collective-permute-start | bytes 221192 | tf_op jit(solution)/shard_map/ppermute | solution.py:390
  27.3 5.0 %collective-permute-start.6 = (f32[80,128]{1,0:T(8,128)S(1)}, f32[80,128]{1,0:T(8,128)S(1)}, u32[]{:S(2)}, u32[]{:S(2)}) collective-permute-start(f32[80,128]{1,0:T(8,128)S(1)} %add_add_fusion.1), channel_id=1, source_target_pairs={{0,2},{1,3},{2,0},{3,1},{4,6},{5,7},{6,4},{7,5},{8,10},{9,11},{10,... | collective-permute-start | bytes 122888 | tf_op jit(solution)/shard_map/ppermute | solution.py:390
  28.1 6.2 %collective-permute-start.8 = (bf16[32,16,128]{2,1,0:T(8,128)(2,1)S(1)}, bf16[32,16,128]{2,1,0:T(8,128)(2,1)S(1)}, u32[]{:S(2)}, u32[]{:S(2)}) collective-permute-start(bf16[32,16,128]{2,1,0:T(8,128)(2,1)S(1)} %get-tuple-element.35), channel_id=1, source_target_pairs={{0,8},{8,0},{16,24},{24,16},{1,9},{9,1},{17,25},{25,17},{2,10},{10... | collective-permute-start | bytes 393224 | tf_op jit(solution)/shard_map/ppermute | solution.py:390
  29.0 5.4 %collective-permute-start.9 = (bf16[32,16,128]{2,1,0:T(8,128)(2,1)S(1)}, bf16[32,16,128]{2,1,0:T(8,128)(2,1)S(1)}, u32[]{:S(2)}, u32[]{:S(2)}) collective-permute-start(bf16[32,16,128]{2,1,0:T(8,128)(2,1)S(1)} %get-tuple-element.36), channel_id=1, source_target_pairs={{0,1},{1,0},{2,3},{3,2},{8,16},{9,17},{10,18},{11,19},{16,8},{17,9... | collective-permute-start | bytes 393224 | tf_op jit(solution)/shard_map/ppermute | solution.py:412
  32.9 1.3 %collective-permute-start.7 = (f32[80,128]{1,0:T(8,128)S(1)}, f32[80,128]{1,0:T(8,128)S(1)}, u32[]{:S(2)}, u32[]{:S(2)}) collective-permute-start(f32[80,128]{1,0:T(8,128)S(1)} %fusion.1.mine), channel_id=1, source_target_pairs={{0,4},{4,0},{1,5},{5,1},{2,6},{6,2},{3,7},{7,3},{8,12},{12,8},{9,1... | collective-permute-start | bytes 122888 | tf_op jit(solution)/shard_map/ppermute | solution.py:390
  46.6 8.9 %collective-permute-start.10 = (bf16[32,16,128]{2,1,0:T(8,128)(2,1)S(1)}, bf16[32,16,128]{2,1,0:T(8,128)(2,1)S(1)}, u32[]{:S(2)}, u32[]{:S(2)}) collective-permute-start(bf16[32,16,128]{2,1,0:T(8,128)(2,1)S(1)} %get-tuple-element.39), channel_id=1, source_target_pairs={{0,8},{8,0},{16,24},{24,16},{1,9},{9,1},{17,25},{25,17},{2,10},{10... | collective-permute-start | bytes 393224 | tf_op jit(solution)/shard_map/ppermute | solution.py:390
  48.1 7.4 %collective-permute-start.11 = (bf16[32,16,128]{2,1,0:T(8,128)(2,1)S(1)}, bf16[32,16,128]{2,1,0:T(8,128)(2,1)S(1)}, u32[]{:S(2)}, u32[]{:S(2)}) collective-permute-start(bf16[32,16,128]{2,1,0:T(8,128)(2,1)S(1)} %get-tuple-element.40), channel_id=1, source_target_pairs={{0,1},{1,0},{2,3},{3,2},{8,16},{9,17},{10,18},{11,19},{16,8},{17,9... | collective-permute-start | bytes 393224 | tf_op jit(solution)/shard_map/ppermute | solution.py:412
  49.4 6.1 %collective-permute-start.12 = (f32[128,128]{1,0:T(8,128)S(1)}, f32[128,128]{1,0:T(8,128)S(1)}, u32[]{:S(2)}, u32[]{:S(2)}) collective-permute-start(f32[128,128]{1,0:T(8,128)S(1)} %get-tuple-element.41), channel_id=1, source_target_pairs={{0,4},{4,0},{1,5},{5,1},{2,6},{6,2},{3,7},{7,3},{8,12},{12,8},{9,1... | collective-permute-start | bytes 196616 | tf_op jit(solution)/shard_map/ppermute | solution.py:390
  49.4 6.1 %collective-permute-start.14 = (f32[64,128]{1,0:T(8,128)S(1)}, f32[64,128]{1,0:T(8,128)S(1)}, u32[]{:S(2)}, u32[]{:S(2)}) collective-permute-start(f32[64,128]{1,0:T(8,128)S(1)} %get-tuple-element.42), channel_id=1, source_target_pairs={{0,8},{8,0},{16,24},{24,16},{1,2},{9,10},{17,18},{25,26},{2,1},{10... | collective-permute-start | bytes 98312 | tf_op jit(solution)/shard_map/ppermute | solution.py:412
  50.2 5.3 %collective-permute-start.13 = (f32[64,128]{1,0:T(8,128)S(1)}, f32[64,128]{1,0:T(8,128)S(1)}, u32[]{:S(2)}, u32[]{:S(2)}) collective-permute-start(f32[64,128]{1,0:T(8,128)S(1)} %get-tuple-element.42), channel_id=1, source_target_pairs={{0,1},{1,0},{2,3},{3,2},{4,5},{5,4},{6,7},{7,6},{8,9},{9,8},{10,11... | collective-permute-start | bytes 98312 | tf_op jit(solution)/shard_map/ppermute | solution.py:390
  68.3 1.3 %collective-permute-start.15 = (f32[208,128]{1,0:T(8,128)S(1)}, f32[208,128]{1,0:T(8,128)S(1)}, u32[]{:S(2)}, u32[]{:S(2)}) collective-permute-start(f32[208,128]{1,0:T(8,128)S(1)} %get-tuple-element.44), channel_id=1, source_target_pairs={{0,4},{4,0},{1,5},{5,1},{2,6},{6,2},{3,7},{7,3},{8,12},{12,8},{9,1... | collective-permute-start | bytes 319496 | tf_op jit(solution)/shard_map/ppermute | solution.py:390
  69.6 4.0 %collective-permute-start.18 = (f32[80,128]{1,0:T(8,128)S(1)}, f32[80,128]{1,0:T(8,128)S(1)}, u32[]{:S(2)}, u32[]{:S(2)}) collective-permute-start(f32[80,128]{1,0:T(8,128)S(1)} %slice_add_fusion.2), channel_id=1, source_target_pairs={{0,16},{8,24},{16,0},{24,8},{1,17},{9,25},{17,1},{25,9},{2,18},{10... | collective-permute-start | bytes 122888 | tf_op jit(solution)/shard_map/ppermute | solution.py:390
  70.7 4.9 %collective-permute-start.17 = (f32[80,128]{1,0:T(8,128)S(1)}, f32[80,128]{1,0:T(8,128)S(1)}, u32[]{:S(2)}, u32[]{:S(2)}) collective-permute-start(f32[80,128]{1,0:T(8,128)S(1)} %slice_add_fusion.2), channel_id=1, source_target_pairs={{0,24},{8,16},{16,8},{24,0},{1,25},{9,17},{17,9},{25,1},{2,26},{10... | collective-permute-start | bytes 122888 | tf_op jit(solution)/shard_map/ppermute | solution.py:390
  72.1 4.0 %collective-permute-start.16 = (f32[80,128]{1,0:T(8,128)S(1)}, f32[80,128]{1,0:T(8,128)S(1)}, u32[]{:S(2)}, u32[]{:S(2)}) collective-permute-start(f32[80,128]{1,0:T(8,128)S(1)} %slice_add_fusion.2), channel_id=1, source_target_pairs={{0,8},{8,0},{16,24},{24,16},{1,9},{9,1},{17,25},{25,17},{2,10},{10... | collective-permute-start | bytes 122888 | tf_op jit(solution)/shard_map/ppermute | solution.py:390
  76.1 7.6 %collective-permute-start.20 = (f32[144,128]{1,0:T(8,128)S(1)}, f32[144,128]{1,0:T(8,128)S(1)}, u32[]{:S(2)}, u32[]{:S(2)}) collective-permute-start(f32[144,128]{1,0:T(8,128)S(1)} %constant_dynamic-update-slice_fusion.2), channel_id=1, source_target_pairs={{0,3},{1,2},{2,1},{3,0},{4,7},{5,6},{6,5},{7,4},{8,11},{9,10},{10,... | collective-permute-start | bytes 221192 | tf_op jit(solution)/shard_map/ppermute | solution.py:390
  78.2 6.2 %collective-permute-start.19 = (f32[144,128]{1,0:T(8,128)S(1)}, f32[144,128]{1,0:T(8,128)S(1)}, u32[]{:S(2)}, u32[]{:S(2)}) collective-permute-start(f32[144,128]{1,0:T(8,128)S(1)} %constant_dynamic-update-slice_fusion.2), channel_id=1, source_target_pairs={{0,1},{1,0},{2,3},{3,2},{4,5},{5,4},{6,7},{7,6},{8,9},{9,8},{10,11... | collective-permute-start | bytes 221192 | tf_op jit(solution)/shard_map/ppermute | solution.py:390
  78.8 5.0 %collective-permute-start.21 = (f32[80,128]{1,0:T(8,128)S(1)}, f32[80,128]{1,0:T(8,128)S(1)}, u32[]{:S(2)}, u32[]{:S(2)}) collective-permute-start(f32[80,128]{1,0:T(8,128)S(1)} %add_add_fusion), channel_id=1, source_target_pairs={{0,2},{1,3},{2,0},{3,1},{4,6},{5,7},{6,4},{7,5},{8,10},{9,11},{10,... | collective-permute-start | bytes 122888 | tf_op jit(solution)/shard_map/ppermute | solution.py:390
  80.6 5.1 %collective-permute-start.23 = (bf16[32,16,128]{2,1,0:T(8,128)(2,1)S(1)}, bf16[32,16,128]{2,1,0:T(8,128)(2,1)S(1)}, u32[]{:S(2)}, u32[]{:S(2)}) collective-permute-start(bf16[32,16,128]{2,1,0:T(8,128)(2,1)S(1)} %get-tuple-element.50), channel_id=1, source_target_pairs={{0,8},{8,0},{16,24},{24,16},{1,9},{9,1},{17,25},{25,17},{2,10},{10... | collective-permute-start | bytes 393224 | tf_op jit(solution)/shard_map/ppermute | solution.py:390
  81.6 5.0 %collective-permute-start.24 = (bf16[32,16,128]{2,1,0:T(8,128)(2,1)S(1)}, bf16[32,16,128]{2,1,0:T(8,128)(2,1)S(1)}, u32[]{:S(2)}, u32[]{:S(2)}) collective-permute-start(bf16[32,16,128]{2,1,0:T(8,128)(2,1)S(1)} %get-tuple-element.51), channel_id=1, source_target_pairs={{0,1},{1,0},{2,3},{3,2},{8,16},{9,17},{10,18},{11,19},{16,8},{17,9... | collective-permute-start | bytes 393224 | tf_op jit(solution)/shard_map/ppermute | solution.py:412
  84.4 1.3 %collective-permute-start.22 = (f32[80,128]{1,0:T(8,128)S(1)}, f32[80,128]{1,0:T(8,128)S(1)}, u32[]{:S(2)}, u32[]{:S(2)}) collective-permute-start(f32[80,128]{1,0:T(8,128)S(1)} %fusion.mine), channel_id=1, source_target_pairs={{0,4},{4,0},{1,5},{5,1},{2,6},{6,2},{3,7},{7,3},{8,12},{12,8},{9,1... | collective-permute-start | bytes 122888 | tf_op jit(solution)/shard_map/ppermute | solution.py:390
